TPU v7x, 32 devices: a whole 2x2x4 slice. The times are simulated.
32 devices in a mesh: row: 8 (over z, y), col: 4 (over x, core).
Axes of the slice: x: 2, y: 2, z: 4, core: 2. Of those that a mesh axis runs over, the one named last changes fastest.
Arguments:
- covariance: bfloat16 [28672, 28672], P('row', 'col'), may hold values from -1 to 8, as said below
- right_side: float32 [28672, 256], P(('col', 'row')), may hold values from -50 to 50
Outputs:
- solution: float32 [28672, 256], P(('col', 'row'))
- residual: float32 [28672, 256], P(('col', 'row'))
- direction: float32 [28672, 256], P(('col', 'row'))
Inputs may be any that keep to these rules, and one draw needn't show every extreme that they name: `covariance`: symmetric and positive definite, with condition number under 100.
All inputs are finite; a program needn't handle non-finite values.
Results may differ from a plain program's by a relative error of at most 0.0158.
Values may be sent and summed in bfloat16 or wider, within the bound.
No kernel may reach another device: no remote copies, remote signals or barrier semaphores. Data moves between devices by JAX's collectives and lax.ppermute only.
A program may use at most 128 MiB of HBM per device.

v0:
```python
import jax
import jax.numpy as jnp
from jax import lax
from jax.sharding import PartitionSpec as P

ITERS = 3


HIGHEST_PRECISION = lax.Precision.HIGHEST


def broadcast(block, axis, owner):
    block = jnp.where(lax.axis_index(axis) == owner, block, jnp.zeros_like(block))
    return lax.psum(block, axis)


def inner_product(left_block, right_block):
    return lax.dot_general(
        left_block,
        right_block,
        (((0,), (0,)), ((), ())),
        precision=HIGHEST_PRECISION,
        preferred_element_type=jnp.float32,
    )


def apply_small(block, coeffs):
    return jnp.dot(block, coeffs, precision=HIGHEST_PRECISION, preferred_element_type=jnp.float32)


def symmetric_part(matrix):
    return 0.5 * (matrix + matrix.T)


def solve_spd(matrix, rhs_block):
    factor = jnp.linalg.cholesky(matrix)
    return jax.scipy.linalg.cho_solve((factor, True), rhs_block)


def gram_total(pieces):
    return lax.psum(pieces, ("row", "col"))


def row_block(column_rows):
    fold_ratio = lax.axis_size("row") // lax.axis_size("col")
    row_index = lax.axis_index("row")
    block_rows = column_rows.shape[0] // fold_ratio
    selected = lax.dynamic_slice_in_dim(
        column_rows, row_index % fold_ratio * block_rows, block_rows, 0
    )
    return broadcast(selected, "col", row_index // fold_ratio)


def body(covariance, right_side):
    residual = right_side
    solution = jnp.zeros_like(residual)
    direction = residual
    norm_now = gram_total((inner_product(residual, residual),))[0]
    for iteration in range(ITERS):
        lowered = direction.astype(jnp.bfloat16)
        column_rows = lax.all_gather(lowered, "row", axis=0, tiled=True)
        own_rows = row_block(column_rows)
        image = lax.psum_scatter(
            lax.dot_general(
                covariance, own_rows, (((0,), (0,)), ((), ())), preferred_element_type=jnp.float32
            ),
            "row",
            scatter_dimension=0,
            tiled=True,
        )
        curv_sum, cross_sum, square_sum = gram_total(
            (
                inner_product(direction, image),
                inner_product(image, residual),
                inner_product(image, image),
            )
        )
        curvature = symmetric_part(curv_sum)
        alpha = solve_spd(curvature, norm_now)
        solution = solution + apply_small(direction, alpha)
        residual = residual - apply_small(image, alpha)
        alpha_cross = apply_small(alpha.T, cross_sum)
        quad_term = apply_small(apply_small(alpha.T, square_sum), alpha)
        norm_next = symmetric_part(norm_now - alpha_cross - alpha_cross.T + quad_term)
        beta = solve_spd(norm_now, norm_next)
        direction = residual + apply_small(direction, beta)
        norm_now = norm_next
    return (solution, residual, direction)


def solution(mesh):
    return jax.shard_map(
        body,
        mesh=mesh,
        in_specs=(P("row", "col"), P(("col", "row"), None)),
        out_specs=(P(("col", "row"), None), P(("col", "row"), None), P(("col", "row"), None)),
        check_vma=False,
    )
```

profile of v0, /device:TPU:1, one launch (start us, length us, event | category | flops | bytes accessed | tf_op | source)
XLA Modules:
  0.0 1556.7 jit_solution(6646963787490742215)
XLA Ops:
  9.3 69.4 %all-gather.4.cloned.1.call-done = bf16[7168,256]{1,0:T(8,128)(2,1)} async-done(((bf16[896,256]{1,0:T(8,128)(2,1)}), bf16[7168,256]{1,0:T(8,128)(2,1)}) %all-gather.4.cloned.1.call-update) | async-done | bytes 3670032 | tf_op jit(solution)/shard_map/all_gather | solution.py:61
  81.8 46.6 %all-reduce.11.cloned.1.call-done = bf16[3584,256]{1,0:T(8,128)(2,1)} async-done(((bf16[3584,256]{1,0:T(8,128)(2,1)}), bf16[3584,256]{1,0:T(8,128)(2,1)}) %all-reduce.11.cloned.1.call-update) | async-done | bytes 1835024 | tf_op jit(solution)/shard_map/psum | solution.py:14
  128.4 25.3 %convolution_bitcast_fusion.2 = f32[7168,256]{0,1:T(8,128)} fusion(bf16[3584,256]{1,0:T(8,128)(2,1)} %all-reduce.11.cloned.1.call-done, bf16[3584,7168]{1,0:T(8,128)(2,1)} %param.5), kind=kOutput, calls=%fused_computation.14 | convolution fusion | flops 13153337344 | bytes 60555264 | tf_op jit(solution)/shard_map/dot_general | solution.py:64
  157.3 128.5 %reduce-scatter.4.cloned.1.call-done = f32[896,256]{0,1:T(8,128)} async-done(((f32[7168,256]{0,1:T(8,128)}), f32[896,256]{0,1:T(8,128)}) %reduce-scatter.4.cloned.1.call-update) | async-done | bytes 917520 | tf_op jit(solution)/shard_map/reduce_scatter | solution.py:63
  291.2 130.5 %all-reduce.21.cloned.1.call-done = (f32[256,256]{1,0:T(8,128)}, f32[256,256]{1,0:T(8,128)}, f32[256,256]{1,0:T(8,128)}, f32[256,256]{1,0:T(8,128)}) async-done(((f32[256,256]{1,0:T(8,128)}, f32[256,256]{1,0:T(8,128)}, f32[256,256]{1,0:T(8,128)}, f32[256,256]{1,0:T(8,128)}), (f32[256,256]{1,0:T(8,128)}, f32[256,256]{1,0:T(8,128)}, f32[256,256]{1,0:T(8,128)}, ...) | async-done | bytes 1048592 | tf_op jit(solution)/shard_map/psum | solution.py:41
  425.9 11.7 cholesky.298
  448.0 11.7 cholesky.315
  466.4 19.8 %custom-call.24 = f32[2,128,128]{1,2,0:T(8,128)S(1)} custom-call(f32[2,128,128]{2,1,0:T(8,128)S(1)} %get-tuple-element.43), custom_call_target="InvertDiagBlocksLowerTriangular" | custom-call | tf_op jit(solution)/shard_map/jit(_cho_solve)/triangular_solve | solution.py:37
  494.5 11.7 cholesky.332
  516.7 11.9 cholesky.349
  535.3 19.7 %custom-call.26 = f32[2,128,128]{1,2,0:T(8,128)S(1)} custom-call(f32[2,128,128]{2,1,0:T(8,128)S(1)} %get-tuple-element.44), custom_call_target="InvertDiagBlocksLowerTriangular" | custom-call | tf_op jit(solution)/shard_map/jit(_cho_solve)/triangular_solve | solution.py:37
  560.6 65.9 %all-gather.6.cloned.1.call-done = bf16[7168,256]{1,0:T(8,128)(2,1)} async-done(((bf16[896,256]{1,0:T(8,128)(2,1)}), bf16[7168,256]{1,0:T(8,128)(2,1)}) %all-gather.6.cloned.1.call-update) | async-done | bytes 3670032 | tf_op jit(solution)/shard_map/all_gather | solution.py:61
  629.6 46.6 %all-reduce.13.cloned.1.call-done = bf16[3584,256]{1,0:T(8,128)(2,1)} async-done(((bf16[3584,256]{1,0:T(8,128)(2,1)}), bf16[3584,256]{1,0:T(8,128)(2,1)}) %all-reduce.13.cloned.1.call-update) | async-done | bytes 1835024 | tf_op jit(solution)/shard_map/psum | solution.py:14
  676.2 25.3 %convolution_bitcast_fusion.1 = f32[7168,256]{0,1:T(8,128)} fusion(bf16[3584,256]{1,0:T(8,128)(2,1)} %all-reduce.13.cloned.1.call-done, bf16[3584,7168]{1,0:T(8,128)(2,1)} %param.5), kind=kOutput, calls=%fused_computation.13 | convolution fusion | flops 13153337344 | bytes 60555264 | tf_op jit(solution)/shard_map/dot_general | solution.py:64
  702.3 11.7 cholesky.400
  724.4 11.7 cholesky.417
  739.4 94.2 %reduce-scatter.6.cloned.1.call-done = f32[896,256]{0,1:T(8,128)} async-done(((f32[7168,256]{0,1:T(8,128)}), f32[896,256]{0,1:T(8,128)}) %reduce-scatter.6.cloned.1.call-update) | async-done | bytes 917520 | tf_op jit(solution)/shard_map/reduce_scatter | solution.py:63
  845.4 20.3 %custom-call.30 = f32[2,128,128]{1,2,0:T(8,128)} custom-call(f32[2,128,128]{2,1,0:T(8,128)S(1)} %get-tuple-element.46), custom_call_target="InvertDiagBlocksLowerTriangular" | custom-call | tf_op jit(solution)/shard_map/jit(_cho_solve)/triangular_solve | solution.py:37
  865.7 105.2 %all-reduce.19.cloned.1.call-done = (f32[256,256]{1,0:T(8,128)}, f32[256,256]{1,0:T(8,128)}, f32[256,256]{1,0:T(8,128)}) async-done(((f32[256,256]{1,0:T(8,128)}, f32[256,256]{1,0:T(8,128)}, f32[256,256]{1,0:T(8,128)}), (f32[256,256]{1,0:T(8,128)}, f32[256,256]{1,0:T(8,128)}, f32[256,256]{1,0:T(8,128)})) %all-reduce.19.cloned.1.call-update) | async-done | bytes 786448 | tf_op jit(solution)/shard_map/psum | solution.py:41
  973.9 11.7 cholesky.366
  997.6 11.7 cholesky.383
  1016.0 20.1 %custom-call.28 = f32[2,128,128]{1,2,0:T(8,128)S(1)} custom-call(f32[2,128,128]{2,1,0:T(8,128)S(1)} %get-tuple-element.45), custom_call_target="InvertDiagBlocksLowerTriangular" | custom-call | tf_op jit(solution)/shard_map/jit(_cho_solve)/triangular_solve | solution.py:37
  1052.3 65.8 %all-gather.8.cloned.1.call-done = bf16[7168,256]{1,0:T(8,128)(2,1)} async-done(((bf16[896,256]{1,0:T(8,128)(2,1)}), bf16[7168,256]{1,0:T(8,128)(2,1)}) %all-gather.8.cloned.1.call-update) | async-done | bytes 3670032 | tf_op jit(solution)/shard_map/all_gather | solution.py:61
  1121.3 46.6 %all-reduce.15.cloned.1.call-done = bf16[3584,256]{1,0:T(8,128)(2,1)} async-done(((bf16[3584,256]{1,0:T(8,128)(2,1)}), bf16[3584,256]{1,0:T(8,128)(2,1)}) %all-reduce.15.cloned.1.call-update) | async-done | bytes 1835024 | tf_op jit(solution)/shard_map/psum | solution.py:14
  1167.9 25.3 %convolution_bitcast_fusion = f32[7168,256]{0,1:T(8,128)} fusion(bf16[3584,256]{1,0:T(8,128)(2,1)} %all-reduce.15.cloned.1.call-done, bf16[3584,7168]{1,0:T(8,128)(2,1)} %param.5), kind=kOutput, calls=%fused_computation.12 | convolution fusion | flops 13153337344 | bytes 60555264 | tf_op jit(solution)/shard_map/dot_general | solution.py:64
  1196.4 11.7 cholesky.468
  1218.5 11.7 cholesky.485
  1233.8 91.4 %reduce-scatter.8.cloned.1.call-done = f32[896,256]{0,1:T(8,128)} async-done(((f32[7168,256]{0,1:T(8,128)}), f32[896,256]{0,1:T(8,128)}) %reduce-scatter.8.cloned.1.call-update) | async-done | bytes 917520 | tf_op jit(solution)/shard_map/reduce_scatter | solution.py:63
  1338.4 20.3 %custom-call.34 = f32[2,128,128]{1,2,0:T(8,128)} custom-call(f32[2,128,128]{2,1,0:T(8,128)S(1)} %get-tuple-element.48), custom_call_target="InvertDiagBlocksLowerTriangular" | custom-call | tf_op jit(solution)/shard_map/jit(_cho_solve)/triangular_solve | solution.py:37
  1362.2 100.1 %all-reduce.17.cloned.1.call-done = (f32[256,256]{1,0:T(8,128)}, f32[256,256]{1,0:T(8,128)}, f32[256,256]{1,0:T(8,128)}) async-done(((f32[256,256]{1,0:T(8,128)}, f32[256,256]{1,0:T(8,128)}, f32[256,256]{1,0:T(8,128)}), (f32[256,256]{1,0:T(8,128)}, f32[256,256]{1,0:T(8,128)}, f32[256,256]{1,0:T(8,128)})) %all-reduce.17.cloned.1.call-update) | async-done | bytes 786448 | tf_op jit(solution)/shard_map/psum | solution.py:41
  1489.0 11.7 cholesky.451
  1508.4 19.8 %custom-call.32 = f32[2,128,128]{1,2,0:T(8,128)S(1)} custom-call(f32[2,128,128]{2,1,0:T(8,128)S(1)} %get-tuple-element.47), custom_call_target="InvertDiagBlocksLowerTriangular" | custom-call | tf_op jit(solution)/shard_map/jit(_cho_solve)/triangular_solve | solution.py:37
  (274 shorter events, 243.3 us)
Async XLA Ops:
  7.2 71.5 %all-gather.4.cloned.1.call-start = ((), (), s32[]{:S(2)}) async-start(), calls=%async_computation.3 | async-start | bytes 4128768 | tf_op jit(solution)/shard_map/all_gather | solution.py:61
  9.2 119.2 %all-reduce.11.cloned.1.call-start = ((), (), s32[]{:S(2)}) async-start(), calls=%async_computation.4 | async-start | bytes 3670016 | tf_op jit(solution)/shard_map/psum | solution.py:14
  81.8 204.1 %reduce-scatter.4.cloned.1.call-start = ((), (), s32[]{:S(2)}) async-start(), calls=%async_computation.5 | async-start | bytes 8257536 | tf_op jit(solution)/shard_map/reduce_scatter | solution.py:63
  153.8 1.2 copy-start
  153.8 267.9 %all-reduce.21.cloned.1.call-start = ((), (), s32[]{:S(2)}) async-start(), calls=%async_computation.14 | async-start | bytes 2097152 | tf_op jit(solution)/shard_map/psum | solution.py:41
  285.8 3.1 copy-start.3
  288.1 2.6 copy-start.12
  290.7 335.8 %all-gather.6.cloned.1.call-start = ((), (), s32[]{:S(2)}) async-start(), calls=%async_computation.6 | async-start | bytes 4128768 | tf_op jit(solution)/shard_map/all_gather | solution.py:61
  425.8 60.5 %copy-start.8 = (f32[256,256]{1,0:T(8,128)S(1)}, f32[256,256]{1,0:T(8,128)}, u32[]{:S(2)}) copy-start(f32[256,256]{1,0:T(8,128)} %get-tuple-element.106) | copy-start | bytes 786436
  493.3 22.7 %copy-start.17 = (f32[256,256]{0,1:T(8,128)S(1)}, f32[256,256]{0,1:T(8,128)}, u32[]{:S(2)}) copy-start(f32[256,256]{0,1:T(8,128)} %get-tuple-element.162) | copy-start | bytes 786436
  558.5 278.4 %copy-start.4 = (f32[896,256]{1,0:T(8,128)}, f32[896,256]{1,0:T(8,128)S(1)}, u32[]{:S(2)}) copy-start(f32[896,256]{1,0:T(8,128)S(1)} %convolution_subtract_fusion.2) | copy-start | bytes 2752516
  560.5 115.7 %all-reduce.13.cloned.1.call-start = ((), (), s32[]{:S(2)}) async-start(), calls=%async_computation.7 | async-start | bytes 3670016 | tf_op jit(solution)/shard_map/psum | solution.py:14
  629.6 204.0 %reduce-scatter.6.cloned.1.call-start = ((), (), s32[]{:S(2)}) async-start(), calls=%async_computation.8 | async-start | bytes 8257536 | tf_op jit(solution)/shard_map/reduce_scatter | solution.py:63
  701.6 269.3 %all-reduce.19.cloned.1.call-start = ((), (), s32[]{:S(2)}) async-start(), calls=%async_computation.13 | async-start | bytes 1572864 | tf_op jit(solution)/shard_map/psum | solution.py:41
  833.6 3.3 copy-start.2
  833.6 5.2 copy-start.6
  838.8 2.4 copy-start.13
  841.2 276.9 %all-gather.8.cloned.1.call-start = ((), (), s32[]{:S(2)}) async-start(), calls=%async_computation.9 | async-start | bytes 4128768 | tf_op jit(solution)/shard_map/all_gather | solution.py:61
  973.2 0.7 copy-start.15
  1044.4 4.3 copy-start.19
  1044.4 4.6 copy-start.5
  1048.3 2.2 copy-start.7
  1052.3 115.6 %all-reduce.15.cloned.1.call-start = ((), (), s32[]{:S(2)}) async-start(), calls=%async_computation.10 | async-start | bytes 3670016 | tf_op jit(solution)/shard_map/psum | solution.py:14
  1121.2 204.0 %reduce-scatter.8.cloned.1.call-start = ((), (), s32[]{:S(2)}) async-start(), calls=%async_computation.11 | async-start | bytes 8257536 | tf_op jit(solution)/shard_map/reduce_scatter | solution.py:63
  1193.2 269.0 %all-reduce.17.cloned.1.call-start = ((), (), s32[]{:S(2)}) async-start(), calls=%async_computation.12 | async-start | bytes 1572864 | tf_op jit(solution)/shard_map/psum | solution.py:41
  1325.2 3.3 copy-start.1
  1464.5 0.7 copy-start.16
  1501.4 2.0 copy-start.14
  1528.3 1.9 copy-start.9
  1530.2 4.4 copy-start.20
  1540.8 3.6 copy-start.18
  1547.8 1.8 copy-start.10
  (1 other events, 0.7 us)
Sparse Core Ops, SparseCore 0:
  10.8 67.8 all-gather.3
  81.9 46.4 all-reduce.10
  153.9 131.8 reduce-scatter.3
  291.8 129.8 all-reduce.20
  560.6 65.7 all-gather.5
  629.7 46.5 all-reduce.12
  701.7 131.8 reduce-scatter.5
  841.3 129.5 all-reduce.18
  1052.4 65.6 all-gather.7
  1121.3 46.4 all-reduce.14
  1193.3 131.8 reduce-scatter.7
  1332.7 129.5 all-reduce.16
where the time goes:
time: 1570 us; the launch traced here: 1560 us
  waiting for transfers between devices  991 us (63%)
  other arithmetic  346 us (22%)
  matrix products  153 us (10%)
  local copies, waits for them, and re-layouts  41.3 us (3%)
  between operations  23.2 us (1%)
    psum x3, waiting for transfers between devices, gram_total(): return lax.psum(pieces, ('row', 'col'))  336 us
    reduce_scatter x3, waiting for transfers between devices, body(): lax.psum_scatter(lax.dot_general(covariance, own_rows, (((0,), (0,)), (()...  314 us
    another operation x42, other arithmetic, solve_spd(): factor = jnp.linalg.cholesky(matrix)  208 us
    all_gather x3, waiting for transfers between devices, body(): column_rows = lax.all_gather(lowered, 'row', axis=0, tiled=True)  201 us
    psum x3, waiting for transfers between devices, broadcast(): return lax.psum(block, axis)  140 us
    another operation x13, other arithmetic, solve_spd(): return jax.scipy.linalg.cho_solve((factor, True), rhs_block)  123 us
    dot_general x3, matrix products, body(): lax.dot_general(covariance, own_rows, (((0,), (0,)), ((), ())), preferred...  76 us
    dot_general x18, matrix products, apply_small(): jnp.dot(block, coeffs, precision=HIGHEST_PRECISION, preferred_element_typ...  32.8 us
  transfers between devices with their start and end apart: 12, of which 12 were waited for; matrix products, arithmetic and copies ran while one was open for 8% of the time, Pallas kernels for 0%

commit v1 on v0

v1 whole, which is shorter than its diff:
```python
import functools

import jax
import jax.numpy as jnp
import numpy as np
from jax import lax
from jax.experimental import pallas as pl
from jax.experimental.pallas import tpu as pltpu
from jax.sharding import PartitionSpec as P

ITERS = 3
AXES = ("row", "col")
HIGHEST = lax.Precision.HIGHEST
VMEM_LIMIT = 48 * 1024 * 1024
DONE = 1e-13
MAX_SQUARINGS = 48


def dot(left, right):
    return jnp.dot(left, right, precision=HIGHEST, preferred_element_type=jnp.float32)


def send(block, pairs):
    return lax.ppermute(block, AXES, pairs)


def vmem_params(**extra):
    return pltpu.CompilerParams(vmem_limit_bytes=VMEM_LIMIT, **extra)


def bits_of(size, first_stride):
    assert size & (size - 1) == 0
    return [first_stride << b for b in range(size.bit_length() - 1)]


def ring_order(rows):
    fast = 1 << ((rows.bit_length() - 1) // 2)
    slow = rows // fast
    if fast == 1 or slow == 1:
        return list(range(rows))
    cycle = [s * fast for s in range(slow)]
    for s in reversed(range(slow)):
        lane = range(1, fast) if (slow - 1 - s) % 2 == 0 else reversed(range(1, fast))
        cycle += [s * fast + f for f in lane]
    return cycle


def chunk_kernel(blocks, has_base, index_ref, *refs):
    covs, parts = refs[:blocks], refs[blocks : 2 * blocks]
    out = refs[-1]
    total = refs[2 * blocks][...] if has_base else None
    for cov, part in zip(covs, parts):
        term = jnp.dot(cov[...], part[...], preferred_element_type=jnp.float32)
        total = term if total is None else total + term
    out[...] = total


def add_chunks(covariance, row_blocks, owners, parts, base, height):
    blocks = len(parts)
    depth, edits = parts[0].shape
    count = row_blocks.shape[0]
    index = jnp.concatenate([jnp.stack(owners).astype(jnp.int32), row_blocks])
    cov_specs = [
        pl.BlockSpec((height, depth), functools.partial(lambda t, i, ix: (ix[blocks + i], ix[t]), t))
        for t in range(blocks)
    ]
    part_specs = [pl.BlockSpec((depth, edits), lambda i, ix: (0, 0)) for _ in parts]
    row_spec = pl.BlockSpec((height, edits), lambda i, ix: (i, 0))
    has_base = base is not None
    operands = [covariance] * blocks + list(parts) + ([base] if has_base else [])
    return pl.pallas_call(
        functools.partial(chunk_kernel, blocks, has_base),
        grid_spec=pltpu.PrefetchScalarGridSpec(
            num_scalar_prefetch=1,
            grid=(count,),
            in_specs=cov_specs + part_specs + ([row_spec] if has_base else []),
            out_specs=row_spec,
        ),
        out_shape=jax.ShapeDtypeStruct((count * height, edits), jnp.float32),
        input_output_aliases={1 + 2 * blocks: 0} if has_base else {},
        compiler_params=vmem_params(),
        cost_estimate=pl.CostEstimate(
            flops=2 * count * height * depth * blocks * edits,
            bytes_accessed=2 * count * height * depth * blocks,
            transcendentals=0,
        ),
    )(index, *operands)


def partial_image(covariance, lowered, order, cols):
    rows = len(order)
    depth = lowered.shape[0]
    quarter = covariance.shape[0] // cols
    me_row, me_col = lax.axis_index("row"), lax.axis_index("col")
    if depth % 128 or depth % 32 or quarter % 16 or rows % 2:
        whole = lax.all_gather(lowered, "row", axis=0, tiled=True)
        product = jnp.dot(covariance, whole, preferred_element_type=jnp.float32)
        swapped = product.reshape(cols, quarter, -1)[jnp.arange(cols) ^ me_col]
        return swapped.reshape(product.shape)
    split = 2 if quarter % 32 == 0 and quarter > 512 else 1
    height = quarter // split
    lane = jnp.arange(cols * split, dtype=jnp.int32)
    row_blocks = ((lane // split) ^ me_col) * split + lane % split
    place = [order.index(r) for r in range(rows)]
    forward = [
        (r * cols + c, order[(place[r] + 1) % rows] * cols + c) for r in range(rows) for c in range(cols)
    ]
    backward = [(b, a) for a, b in forward]
    cycle, where = jnp.array(order, jnp.int32), jnp.array(place, jnp.int32)[me_row]

    def owner(shift):
        return cycle[(where + shift) % rows]

    ahead = behind = lowered
    held, owners, total = [lowered], [me_row], None
    for step in range(1, rows // 2 + 1):
        if step < rows // 2:
            behind, ahead = send(behind, forward), send(ahead, backward)
            arrived, names = [behind, ahead], [owner(-step), owner(step)]
        else:
            half = depth // 2
            low, high = send(behind[:half], forward), send(ahead[half:], backward)
            arrived, names = [jnp.concatenate([low, high])], [owner(step)]
        total = add_chunks(covariance, row_blocks, owners, held, total, height)
        held, owners = arrived, names
    return add_chunks(covariance, row_blocks, owners, held, total, height)


def exchange_sum(total, cols):
    quarter = total.shape[0] // cols
    pieces = {j: total[j * quarter : (j + 1) * quarter] for j in range(cols)}
    rows = lax.axis_size("row")
    strides = bits_of(cols, 1)
    for bit in strides:
        pairs = [(i, i ^ bit) for i in range(rows * cols)]
        last = bit == strides[-1]
        got = {}
        for j in sorted((j for j in pieces if j & bit), reverse=True):
            block = pieces[j].astype(jnp.bfloat16) if bit > 1 else pieces[j]
            got[j ^ bit] = send(block, pairs)
        if last:
            return pieces[0], got[0]
        pieces = {j: pieces[j] + got[j].astype(jnp.float32) for j in got}
    return pieces[0], jnp.zeros_like(pieces[0])


def gram_kernel(first, own, got, residual, *refs):
    direction = None if first else refs[0]
    image, grams = refs[-2:]
    value = own[...] + got[...].astype(jnp.float32)
    image[...] = value
    order = value.shape[1]
    flipped = value.T
    grams[0:order] = dot(flipped, value)
    grams[order : 2 * order] = dot(flipped, residual[...])
    if first:
        grams[2 * order :] = dot(residual[...].T, residual[...])
    else:
        grams[2 * order :] = dot(flipped, direction[...])


def local_grams(own, got, residual, direction, first):
    rows, edits = own.shape
    operands = [own, got, residual] + ([] if first else [direction])
    return pl.pallas_call(
        functools.partial(gram_kernel, first),
        out_shape=[
            jax.ShapeDtypeStruct((rows, edits), jnp.float32),
            jax.ShapeDtypeStruct((3 * edits, edits), jnp.float32),
        ],
        compiler_params=vmem_params(),
        cost_estimate=pl.CostEstimate(
            flops=36 * rows * edits * edits, bytes_accessed=16 * rows * edits, transcendentals=0
        ),
    )(*operands)


def sum_all(block, rows, cols):
    total = rows * cols
    me = lax.axis_index("row") * cols + lax.axis_index("col")
    strides = bits_of(total, 1)
    for stride in strides:
        pairs = [(i, i ^ stride) for i in range(total)]
        size = block.shape[0] // 2
        digit = (me // stride) % 2
        got = send(lax.dynamic_slice_in_dim(block, (1 - digit) * size, size, 0), pairs)
        block = lax.dynamic_slice_in_dim(block, digit * size, size, 0) + got
    for stride in reversed(strides):
        pairs = [(i, i ^ stride) for i in range(total)]
        digit = (me // stride) % 2
        got = send(block, pairs)
        block = jnp.concatenate([jnp.where(digit == 0, block, got), jnp.where(digit == 0, got, block)])
    return block


def squared_norm(matrix):
    return jnp.sum(matrix * matrix)


def scaled_error(matrix, scale_ref, error_ref):
    order = matrix.shape[0]
    row = lax.broadcasted_iota(jnp.int32, (order, order), 0)
    col = lax.broadcasted_iota(jnp.int32, (order, order), 1)
    eye = jnp.where(row == col, 1.0, 0.0).astype(jnp.float32)
    diagonal = matrix * eye
    across = lax.rsqrt(jnp.sum(diagonal, axis=0, keepdims=True))
    down = lax.rsqrt(jnp.sum(diagonal, axis=1, keepdims=True))
    scale_ref[...] = down
    unit = matrix * across * down
    error = eye - unit
    square = dot(error, error)
    safe = squared_norm(square) < 0.9
    bound = jnp.max(jnp.sum(jnp.abs(unit), axis=1))
    factor = jnp.where(safe, 1.0, 1.0 / bound)
    error_ref[...] = eye - factor * unit
    return factor


def power_solve(matrix, rhs, scale_ref, error_ref, value_ref):
    factor = scaled_error(matrix, scale_ref, error_ref)
    value_ref[...] = factor * scale_ref[...] * rhs

    def step(state):
        count, _ = state
        error = error_ref[...]
        value_ref[...] += dot(error, value_ref[...])
        size = squared_norm(error)
        error_ref[...] = dot(error, error)
        return count + 1, size

    lax.while_loop(lambda s: (s[0] < MAX_SQUARINGS) & (s[1] > DONE), step, (0, jnp.float32(1.0)))
    return scale_ref[...] * value_ref[...]


def solve_kernel(first, grams, norm_in, alpha, beta, norm_out, scale, error, value):
    order = alpha.shape[0]
    square = grams[0:order]
    cross = grams[order : 2 * order]
    norm = grams[2 * order :] if first else norm_in[...]
    curvature = cross if first else grams[2 * order :]
    curvature = 0.5 * (curvature + curvature.T)
    step = power_solve(curvature, norm, scale, error, value)
    alpha[...] = step
    change = dot(step.T, dot(square, step) - 2.0 * cross)
    after = norm + 0.5 * (change + change.T)
    norm_out[...] = after
    beta[...] = power_solve(norm, after, scale, error, value)


def solve_small(grams, norm, first):
    edits = grams.shape[1]
    square = jax.ShapeDtypeStruct((edits, edits), jnp.float32)
    return pl.pallas_call(
        functools.partial(solve_kernel, first),
        out_shape=[square, square, square],
        scratch_shapes=[
            pltpu.VMEM((edits, 1), jnp.float32),
            pltpu.VMEM((edits, edits), jnp.float32),
            pltpu.VMEM((edits, edits), jnp.float32),
        ],
        compiler_params=vmem_params(),
        cost_estimate=pl.CostEstimate(
            flops=200 * edits * edits * edits, bytes_accessed=32 * edits * edits, transcendentals=0
        ),
    )(grams, norm)


def update_kernel(residual, direction, image, alpha, beta, residual_out, direction_out, lowered_out):
    after = residual[...] - dot(image[...], alpha[...])
    residual_out[...] = after
    following = after + dot(direction[...], beta[...])
    direction_out[...] = following
    lowered_out[...] = following.astype(jnp.bfloat16)


def update(residual, direction, image, alpha, beta):
    rows, edits = residual.shape
    full = jax.ShapeDtypeStruct((rows, edits), jnp.float32)
    return pl.pallas_call(
        update_kernel,
        out_shape=[full, full, jax.ShapeDtypeStruct((rows, edits), jnp.bfloat16)],
        compiler_params=vmem_params(),
        cost_estimate=pl.CostEstimate(
            flops=24 * rows * edits * edits, bytes_accessed=22 * rows * edits, transcendentals=0
        ),
    )(residual, direction, image, alpha, beta)


def body(rows, cols, covariance, right_side):
    order = ring_order(rows)
    to_outer = [(k, (k % rows) * cols + k // rows) for k in range(rows * cols)]
    to_inner = [(b, a) for a, b in to_outer]
    residual = direction = right_side
    inner_residual = inner_direction = send(right_side, to_inner)
    lowered = right_side.astype(jnp.bfloat16)
    iterate = norm = None
    for iteration in range(ITERS):
        first, last = iteration == 0, iteration == ITERS - 1
        total = partial_image(covariance, lowered, order, cols)
        own, got = exchange_sum(total, cols)
        inner_image, grams = local_grams(own, got, inner_residual, inner_direction, first)
        image = send(inner_image, to_outer)
        grams = sum_all(grams, rows, cols)
        alpha, beta, norm = solve_small(grams, grams[: grams.shape[1]] if first else norm, first)
        moved = dot(direction, alpha)
        iterate = moved if first else iterate + moved
        residual, direction, lowered = update(residual, direction, image, alpha, beta)
        if not last:
            inner_residual, inner_direction, _ = update(
                inner_residual, inner_direction, inner_image, alpha, beta
            )
    return (iterate, residual, direction)


def solution(mesh):
    place = P(("col", "row"), None)
    return jax.shard_map(
        functools.partial(body, mesh.shape["row"], mesh.shape["col"]),
        mesh=mesh,
        in_specs=(P("row", "col"), place),
        out_specs=(place, place, place),
        check_vma=False,
    )
```

time: 1570 us -> 635 us (0.40)
  waiting for transfers between devices: 991 us -> 274 us
  other arithmetic: 346 us -> 14.9 us
  Pallas kernels: 0 us -> 212 us
  matrix products: 153 us -> 4.97 us
  starting transfers between devices: 1.61 us -> 106 us
  local copies, waits for them, and re-layouts: 41.3 us -> 8.9 us
  between operations: 23.2 us -> 6.51 us
    psum x6 -> x0, waiting for transfers between devices: 476 us -> none  [the longest x3 336 us: gram_total(): return lax.psum(pieces, ('row', 'col'))]
    another operation x55 -> x0, other arithmetic: 331 us -> none  [the longest x42 208 us: solve_spd(): factor = jnp.linalg.cholesky(matrix)]
    reduce_scatter x3 -> x0, waiting for transfers between devices: 314 us -> none  [body(): lax.psum_scatter(lax.dot_general(covariance, own_rows, (((0,), (0,)), (()...]
    ppermute x0 -> x67, waiting for transfers between devices: none -> 274 us  [send(): return lax.ppermute(block, AXES, pairs)]
    pallas_call x0 -> x26, Pallas kernels: none -> 212 us  [the longest x15 132 us: add_chunks(): pl.pallas_call(functools.partial(chunk_kernel, blocks, has_base), grid_sp...]
    all_gather x3 -> x0, waiting for transfers between devices: 201 us -> none  [body(): column_rows = lax.all_gather(lowered, 'row', axis=0, tiled=True)]
    dot_general x30 -> x3, matrix products: 130 us -> 4.97 us  [dot(): jnp.dot(left, right, precision=HIGHEST, preferred_element_type=jnp.float32)]
    ppermute x0 -> x67, starting transfers between devices: none -> 106 us  [send(): return lax.ppermute(block, AXES, pairs)]
  transfers between devices with their start and end apart: 12 -> 67, of which waited for: 12 -> 42; matrix products, arithmetic and copies ran while one was open for 8% -> 3% of each run, Pallas kernels for 0% -> 27%
where the time goes in v1:
time: 635 us; the launch traced here: 626 us
  waiting for transfers between devices  274 us (43%)
  Pallas kernels  212 us (33%)
  starting transfers between devices  106 us (17%)
  other arithmetic  14.9 us (2%)
  local copies, waits for them, and re-layouts  8.9 us (1%)
  between operations  6.51 us (1%)
    ppermute x67, waiting for transfers between devices, send(): return lax.ppermute(block, AXES, pairs)  274 us
    pallas_call x15, Pallas kernels, add_chunks(): pl.pallas_call(functools.partial(chunk_kernel, blocks, has_base), grid_sp...  132 us
    ppermute x67, starting transfers between devices, send(): return lax.ppermute(block, AXES, pairs)  106 us
    pallas_call x3, Pallas kernels, solve_small(): pl.pallas_call(functools.partial(solve_kernel, first), out_shape=[square,...  57.1 us
    pallas_call x5, Pallas kernels, update(): pl.pallas_call(update_kernel, out_shape=[full, full, jax.ShapeDtypeStruct...  13.9 us
  transfers between devices with their start and end apart: 67, of which 42 were waited for; matrix products, arithmetic and copies ran while one was open for 3% of the time, Pallas kernels for 27%

profile of v1, /device:TPU:1, one launch (start us, length us, event | category | flops | bytes accessed | tf_op | source)
XLA Modules:
  0.0 626.4 jit_solution(7635299554620037007)
XLA Ops:
  20.3 7.4 %shard_map.103.refs_4_ = f32[3584,256]{1,0:T(8,128)S(1)} custom-call(s32[9]{0:T(128)S(1)} %get-tuple-element.94.index_ref, bf16[3584,7168]{1,0:T(8,128)(2,1)} %refs_0_.29, bf16[896,256]{1,0:T(8,128)(2,1)S(1)} %convert_element_type.12.refs_1_), custom_call_target="tpu_custom_call" | custom-call | flops 1644167168 | bytes 6422528 | tf_op jit(solution)/shard_map/pallas_call | solution.py:71
  29.2 9.7 %shard_map.104.refs_4_ = f32[3584,256]{1,0:T(8,128)S(1)} custom-call(s32[10]{0:T(128)S(1)} %get-tuple-element.96.index_ref, bf16[3584,7168]{1,0:T(8,128)(2,1)} %refs_0_.29, bf16[3584,7168]{1,0:T(8,128)(2,1)} %refs_0_.29, bf16[896,256]{1,0:T(8,128)(2,1)S(1)} %collective-permute-done.refs_2_, ...), custom_call_target="tpu_custom_call", output_to_operand_aliasing={{}: (5, {})} | custom-call | flops 3288334336 | bytes 12845056 | tf_op jit(solution)/shard_map/pallas_call | solution.py:71
  38.9 9.7 %shard_map.105.refs_4_ = f32[3584,256]{1,0:T(8,128)S(1)} custom-call(s32[10]{0:T(128)S(1)} %get-tuple-element.97.index_ref, bf16[3584,7168]{1,0:T(8,128)(2,1)} %refs_0_.29, bf16[3584,7168]{1,0:T(8,128)(2,1)} %refs_0_.29, bf16[896,256]{1,0:T(8,128)(2,1)S(1)} %collective-permute-done.1.refs_2_, ...), custom_call_target="tpu_custom_call", output_to_operand_aliasing={{}: (5, {})} | custom-call | flops 3288334336 | bytes 12845056 | tf_op jit(solution)/shard_map/pallas_call | solution.py:71
  50.3 9.7 %shard_map.106.refs_2_ = f32[3584,256]{1,0:T(8,128)S(1)} custom-call(s32[10]{0:T(128)S(1)} %get-tuple-element.98.index_ref, bf16[3584,7168]{1,0:T(8,128)(2,1)} %refs_0_.29, bf16[3584,7168]{1,0:T(8,128)(2,1)} %refs_0_.29, bf16[896,256]{1,0:T(8,128)(2,1)S(1)} %collective-permute-done.2.refs_2_, ...), custom_call_target="tpu_custom_call", output_to_operand_aliasing={{}: (5, {})} | custom-call | flops 3288334336 | bytes 12845056 | tf_op jit(solution)/shard_map/pallas_call | solution.py:71
  60.1 7.4 %shard_map.107 = f32[3584,256]{1,0:T(8,128)S(1)} custom-call(s32[9]{0:T(128)S(1)} %get-tuple-element.95.index_ref, bf16[3584,7168]{1,0:T(8,128)(2,1)} %refs_0_.29, bf16[896,256]{1,0:T(8,128)(2,1)S(1)} %pad_maximum_fusion.3.refs_1_, f32[3584,256]{1,0:T(8,128)S(1)} %shard_map.106.refs_2_), custom_call_target="tpu_custom_call", output_to_operand_aliasing={{}: (3, {})} | custom-call | flops 1644167168 | bytes 6422528 | tf_op jit(solution)/shard_map/pallas_call | solution.py:71
  82.4 6.7 %collective-permute-done.11.residual.direction = f32[896,256]{1,0:T(8,128)S(1)} collective-permute-done((f32[896,256]{1,0:T(8,128)S(1)}, f32[896,256]{1,0:T(8,128)S(1)}, u32[]{:S(2)}, u32[]{:S(2)}) %collective-permute-start.11) | collective-permute-done | bytes 917536 | tf_op jit(solution)/shard_map/ppermute | solution.py:24
  89.1 20.3 %collective-permute-done.10.got = bf16[896,256]{1,0:T(8,128)(2,1)S(1)} collective-permute-done((bf16[896,256]{1,0:T(8,128)(2,1)S(1)}, bf16[896,256]{1,0:T(8,128)(2,1)S(1)}, u32[]{:S(2)}, u32[]{:S(2)}) %collective-permute-start.10) | collective-permute-done | bytes 458784 | tf_op jit(solution)/shard_map/ppermute | solution.py:24
  124.5 11.1 %collective-permute-start.14 = (f32[96,256]{1,0:T(8,128)S(1)}, f32[96,256]{1,0:T(8,128)S(1)}, u32[]{:S(2)}, u32[]{:S(2)}) collective-permute-start(f32[96,256]{1,0:T(8,128)S(1)} %constant_dynamic-slice_fusion.12), channel_id=1, source_target_pairs={{0,4},{1,5},{2,6},{3,7},{4,0},{5,1},{6,2},{7,3},{8,12},{9,13},{10,... | collective-permute-start | bytes 294920 | tf_op jit(solution)/shard_map/ppermute | solution.py:24
  162.0 8.8 %collective-permute-start.21 = (f32[384,256]{1,0:T(8,128)}, f32[384,256]{1,0:T(8,128)}, u32[]{:S(2)}, u32[]{:S(2)}) collective-permute-start(f32[384,256]{1,0:T(8,128)} %pad_maximum_fusion.6), channel_id=1, source_target_pairs={{0,1},{1,0},{2,3},{3,2},{4,5},{5,4},{6,7},{7,6},{8,9},{9,8},{10,11... | collective-permute-start | bytes 1179656 | tf_op jit(solution)/shard_map/ppermute | solution.py:24
  175.0 18.9 %shard_map.109 = (f32[256,256]{1,0:T(8,128)S(1)}, f32[256,256]{1,0:T(8,128)S(1)}, f32[256,256]{1,0:T(8,128)S(1)}) custom-call(f32[768,256]{1,0:T(8,128)S(1)} %pad_maximum_fusion.grams, f32[256,256]{1,0:T(8,128)S(1)} %slice.82.norm_in), custom_call_target="tpu_custom_call" | custom-call | flops 3355443200 | bytes 2097152 | tf_op jit(solution)/shard_map/pallas_call | solution.py:253
  193.9 40.7 %collective-permute-done.22.image = f32[896,256]{1,0:T(8,128)} collective-permute-done((f32[896,256]{1,0:T(8,128)S(1)}, f32[896,256]{1,0:T(8,128)}, u32[]{:S(2)}, u32[]{:S(2)}) %collective-permute-start.22) | collective-permute-done | bytes 917536 | tf_op jit(solution)/shard_map/ppermute | solution.py:24
  239.0 8.6 %collective-permute-done.23.refs_2_ = bf16[896,256]{1,0:T(8,128)(2,1)S(1)} collective-permute-done((bf16[896,256]{1,0:T(8,128)(2,1)S(1)}, bf16[896,256]{1,0:T(8,128)(2,1)S(1)}, u32[]{:S(2)}, u32[]{:S(2)}) %collective-permute-start.23) | collective-permute-done | bytes 458784 | tf_op jit(solution)/shard_map/ppermute | solution.py:24
  250.1 7.4 %shard_map.111.refs_4_ = f32[3584,256]{1,0:T(8,128)S(1)} custom-call(s32[9]{0:T(128)S(1)} %get-tuple-element.94.index_ref, bf16[3584,7168]{1,0:T(8,128)(2,1)} %refs_0_.29, bf16[896,256]{1,0:T(8,128)(2,1)S(1)} %get-tuple-element.34.refs_1_), custom_call_target="tpu_custom_call" | custom-call | flops 1644167168 | bytes 6422528 | tf_op jit(solution)/shard_map/pallas_call | solution.py:71
  261.8 9.7 %shard_map.112.refs_4_ = f32[3584,256]{1,0:T(8,128)S(1)} custom-call(s32[10]{0:T(128)S(1)} %get-tuple-element.96.index_ref, bf16[3584,7168]{1,0:T(8,128)(2,1)} %refs_0_.29, bf16[3584,7168]{1,0:T(8,128)(2,1)} %refs_0_.29, bf16[896,256]{1,0:T(8,128)(2,1)S(1)} %collective-permute-done.23.refs_2_, ...), custom_call_target="tpu_custom_call", output_to_operand_aliasing={{}: (5, {})} | custom-call | flops 3288334336 | bytes 12845056 | tf_op jit(solution)/shard_map/pallas_call | solution.py:71
  271.5 9.7 %shard_map.113.refs_4_ = f32[3584,256]{1,0:T(8,128)S(1)} custom-call(s32[10]{0:T(128)S(1)} %get-tuple-element.97.index_ref, bf16[3584,7168]{1,0:T(8,128)(2,1)} %refs_0_.29, bf16[3584,7168]{1,0:T(8,128)(2,1)} %refs_0_.29, bf16[896,256]{1,0:T(8,128)(2,1)S(1)} %collective-permute-done.24.refs_2_, ...), custom_call_target="tpu_custom_call", output_to_operand_aliasing={{}: (5, {})} | custom-call | flops 3288334336 | bytes 12845056 | tf_op jit(solution)/shard_map/pallas_call | solution.py:71
  283.3 9.7 %shard_map.114.refs_2_ = f32[3584,256]{1,0:T(8,128)S(1)} custom-call(s32[10]{0:T(128)S(1)} %get-tuple-element.98.index_ref, bf16[3584,7168]{1,0:T(8,128)(2,1)} %refs_0_.29, bf16[3584,7168]{1,0:T(8,128)(2,1)} %refs_0_.29, bf16[896,256]{1,0:T(8,128)(2,1)S(1)} %collective-permute-done.25.refs_2_, ...), custom_call_target="tpu_custom_call", output_to_operand_aliasing={{}: (5, {})} | custom-call | flops 3288334336 | bytes 12845056 | tf_op jit(solution)/shard_map/pallas_call | solution.py:71
  293.1 7.4 %shard_map.115 = f32[3584,256]{1,0:T(8,128)S(1)} custom-call(s32[9]{0:T(128)S(1)} %get-tuple-element.95.index_ref, bf16[3584,7168]{1,0:T(8,128)(2,1)} %refs_0_.29, bf16[896,256]{1,0:T(8,128)(2,1)S(1)} %pad_maximum_fusion.4.refs_1_, f32[3584,256]{1,0:T(8,128)S(1)} %shard_map.114.refs_2_), custom_call_target="tpu_custom_call", output_to_operand_aliasing={{}: (3, {})} | custom-call | flops 1644167168 | bytes 6422528 | tf_op jit(solution)/shard_map/pallas_call | solution.py:71
  308.1 9.3 %collective-permute-done.33.got = bf16[896,256]{1,0:T(8,128)(2,1)S(1)} collective-permute-done((bf16[896,256]{1,0:T(8,128)(2,1)S(1)}, bf16[896,256]{1,0:T(8,128)(2,1)S(1)}, u32[]{:S(2)}, u32[]{:S(2)}) %collective-permute-start.33) | collective-permute-done | bytes 458784 | tf_op jit(solution)/shard_map/ppermute | solution.py:24
  322.9 6.1 collective-permute-done.35
  354.2 9.3 %collective-permute-start.43 = (f32[384,256]{1,0:T(8,128)S(1)}, f32[384,256]{1,0:T(8,128)S(1)}, u32[]{:S(2)}, u32[]{:S(2)}) collective-permute-start(f32[384,256]{1,0:T(8,128)S(1)} %pad_maximum_fusion.7), channel_id=1, source_target_pairs={{0,1},{1,0},{2,3},{3,2},{4,5},{5,4},{6,7},{7,6},{8,9},{9,8},{10,11... | collective-permute-start | bytes 1179656 | tf_op jit(solution)/shard_map/ppermute | solution.py:24
  365.6 18.9 %shard_map.118 = (f32[256,256]{1,0:T(8,128)S(1)}, f32[256,256]{1,0:T(8,128)S(1)}, f32[256,256]{1,0:T(8,128)S(1)}) custom-call(f32[768,256]{1,0:T(8,128)S(1)} %pad_maximum_fusion.1.grams, f32[256,256]{1,0:T(8,128)S(1)} %get-tuple-element.38.norm_in), custom_call_target="tpu_custom_call" | custom-call | flops 3355443200 | bytes 2097152 | tf_op jit(solution)/shard_map/pallas_call | solution.py:253
  384.4 42.6 %collective-permute-done.44.image = f32[896,256]{1,0:T(8,128)S(1)} collective-permute-done((f32[896,256]{1,0:T(8,128)S(1)}, f32[896,256]{1,0:T(8,128)S(1)}, u32[]{:S(2)}, u32[]{:S(2)}) %collective-permute-start.44) | collective-permute-done | bytes 917536 | tf_op jit(solution)/shard_map/ppermute | solution.py:24
  431.2 8.5 %collective-permute-done.45.refs_2_ = bf16[896,256]{1,0:T(8,128)(2,1)S(1)} collective-permute-done((bf16[896,256]{1,0:T(8,128)(2,1)S(1)}, bf16[896,256]{1,0:T(8,128)(2,1)S(1)}, u32[]{:S(2)}, u32[]{:S(2)}) %collective-permute-start.45) | collective-permute-done | bytes 458784 | tf_op jit(solution)/shard_map/ppermute | solution.py:24
  442.5 7.4 %shard_map.120.refs_4_ = f32[3584,256]{1,0:T(8,128)S(1)} custom-call(s32[9]{0:T(128)S(1)} %get-tuple-element.94.index_ref, bf16[3584,7168]{1,0:T(8,128)(2,1)} %refs_0_.29, bf16[896,256]{1,0:T(8,128)(2,1)S(1)} %get-tuple-element.44.refs_1_), custom_call_target="tpu_custom_call" | custom-call | flops 1644167168 | bytes 6422528 | tf_op jit(solution)/shard_map/pallas_call | solution.py:71
  454.3 9.7 %shard_map.121.refs_4_ = f32[3584,256]{1,0:T(8,128)S(1)} custom-call(s32[10]{0:T(128)S(1)} %get-tuple-element.96.index_ref, bf16[3584,7168]{1,0:T(8,128)(2,1)} %refs_0_.29, bf16[3584,7168]{1,0:T(8,128)(2,1)} %refs_0_.29, bf16[896,256]{1,0:T(8,128)(2,1)S(1)} %collective-permute-done.45.refs_2_, ...), custom_call_target="tpu_custom_call", output_to_operand_aliasing={{}: (5, {})} | custom-call | flops 3288334336 | bytes 12845056 | tf_op jit(solution)/shard_map/pallas_call | solution.py:71
  464.1 9.7 %shard_map.122.refs_4_ = f32[3584,256]{1,0:T(8,128)S(1)} custom-call(s32[10]{0:T(128)S(1)} %get-tuple-element.97.index_ref, bf16[3584,7168]{1,0:T(8,128)(2,1)} %refs_0_.29, bf16[3584,7168]{1,0:T(8,128)(2,1)} %refs_0_.29, bf16[896,256]{1,0:T(8,128)(2,1)S(1)} %collective-permute-done.46.refs_2_, ...), custom_call_target="tpu_custom_call", output_to_operand_aliasing={{}: (5, {})} | custom-call | flops 3288334336 | bytes 12845056 | tf_op jit(solution)/shard_map/pallas_call | solution.py:71
  475.5 9.7 %shard_map.123.refs_2_ = f32[3584,256]{1,0:T(8,128)S(1)} custom-call(s32[10]{0:T(128)S(1)} %get-tuple-element.98.index_ref, bf16[3584,7168]{1,0:T(8,128)(2,1)} %refs_0_.29, bf16[3584,7168]{1,0:T(8,128)(2,1)} %refs_0_.29, bf16[896,256]{1,0:T(8,128)(2,1)S(1)} %collective-permute-done.47.refs_2_, ...), custom_call_target="tpu_custom_call", output_to_operand_aliasing={{}: (5, {})} | custom-call | flops 3288334336 | bytes 12845056 | tf_op jit(solution)/shard_map/pallas_call | solution.py:71
  485.2 7.4 %shard_map.124 = f32[3584,256]{1,0:T(8,128)S(1)} custom-call(s32[9]{0:T(128)S(1)} %get-tuple-element.95.index_ref, bf16[3584,7168]{1,0:T(8,128)(2,1)} %refs_0_.29, bf16[896,256]{1,0:T(8,128)(2,1)S(1)} %pad_maximum_fusion.5.refs_1_, f32[3584,256]{1,0:T(8,128)S(1)} %shard_map.123.refs_2_), custom_call_target="tpu_custom_call", output_to_operand_aliasing={{}: (3, {})} | custom-call | flops 1644167168 | bytes 6422528 | tf_op jit(solution)/shard_map/pallas_call | solution.py:71
  500.2 9.3 %collective-permute-done.55.got = bf16[896,256]{1,0:T(8,128)(2,1)S(1)} collective-permute-done((bf16[896,256]{1,0:T(8,128)(2,1)S(1)}, bf16[896,256]{1,0:T(8,128)(2,1)S(1)}, u32[]{:S(2)}, u32[]{:S(2)}) %collective-permute-start.55) | collective-permute-done | bytes 458784 | tf_op jit(solution)/shard_map/ppermute | solution.py:24
  546.2 9.3 %collective-permute-start.65 = (f32[384,256]{1,0:T(8,128)S(1)}, f32[384,256]{1,0:T(8,128)S(1)}, u32[]{:S(2)}, u32[]{:S(2)}) collective-permute-start(f32[384,256]{1,0:T(8,128)S(1)} %pad_maximum_fusion.8), channel_id=1, source_target_pairs={{0,1},{1,0},{2,3},{3,2},{4,5},{5,4},{6,7},{7,6},{8,9},{9,8},{10,11... | collective-permute-start | bytes 1179656 | tf_op jit(solution)/shard_map/ppermute | solution.py:24
  559.7 19.4 %shard_map.127 = (f32[256,256]{1,0:T(8,128)S(1)}, f32[256,256]{1,0:T(8,128)S(1)}, f32[256,256]{1,0:T(8,128)}) custom-call(f32[768,256]{1,0:T(8,128)S(1)} %pad_maximum_fusion.2.grams, f32[256,256]{1,0:T(8,128)S(1)} %get-tuple-element.48.norm_in), custom_call_target="tpu_custom_call" | custom-call | flops 3355443200 | bytes 2097152 | tf_op jit(solution)/shard_map/pallas_call | solution.py:253
  584.6 36.1 %collective-permute-done.66.image = f32[896,256]{1,0:T(8,128)} collective-permute-done((f32[896,256]{1,0:T(8,128)S(1)}, f32[896,256]{1,0:T(8,128)}, u32[]{:S(2)}, u32[]{:S(2)}) %collective-permute-start.66) | collective-permute-done | bytes 917536 | tf_op jit(solution)/shard_map/ppermute | solution.py:24
  (237 shorter events, 204.0 us)
Async XLA Ops:
  1.9 12.4 %collective-permute-start = (bf16[896,256]{1,0:T(8,128)(2,1)S(1)}, bf16[896,256]{1,0:T(8,128)(2,1)S(1)}, u32[]{:S(2)}, u32[]{:S(2)}) collective-permute-start(bf16[896,256]{1,0:T(8,128)(2,1)S(1)} %convert_element_type.12.refs_1_), channel_id=1, source_target_pairs={{0,8},{1,9},{2,10},{3,11},{4,0},{5,1},{6,2},{7,3},{8,16},{9,17},{1... | collective-permute-start | bytes 1376264 | tf_op jit(solution)/shard_map/ppermute | solution.py:24
  4.0 11.4 %collective-permute-start.4 = (bf16[896,256]{1,0:T(8,128)(2,1)S(1)}, bf16[896,256]{1,0:T(8,128)(2,1)S(1)}, u32[]{:S(2)}, u32[]{:S(2)}) collective-permute-start(bf16[896,256]{1,0:T(8,128)(2,1)S(1)} %convert_element_type.12.refs_1_), channel_id=1, source_target_pairs={{8,0},{9,1},{10,2},{11,3},{0,4},{1,5},{2,6},{3,7},{16,8},{17,9},{1... | collective-permute-start | bytes 1376264 | tf_op jit(solution)/shard_map/ppermute | solution.py:24
  14.2 13.5 %collective-permute-start.1 = (bf16[896,256]{1,0:T(8,128)(2,1)S(1)}, bf16[896,256]{1,0:T(8,128)(2,1)S(1)}, u32[]{:S(2)}, u32[]{:S(2)}) collective-permute-start(bf16[896,256]{1,0:T(8,128)(2,1)S(1)} %collective-permute-done.refs_2_), channel_id=1, source_target_pairs={{0,8},{1,9},{2,10},{3,11},{4,0},{5,1},{6,2},{7,3},{8,16},{9,17},{1... | collective-permute-start | bytes 1376264 | tf_op jit(solution)/shard_map/ppermute | solution.py:24
  15.4 13.5 %collective-permute-start.5 = (bf16[896,256]{1,0:T(8,128)(2,1)S(1)}, bf16[896,256]{1,0:T(8,128)(2,1)S(1)}, u32[]{:S(2)}, u32[]{:S(2)}) collective-permute-start(bf16[896,256]{1,0:T(8,128)(2,1)S(1)} %collective-permute-done.4.refs_3_), channel_id=1, source_target_pairs={{8,0},{9,1},{10,2},{11,3},{0,4},{1,5},{2,6},{3,7},{16,8},{17,9},{1... | collective-permute-start | bytes 1376264 | tf_op jit(solution)/shard_map/ppermute | solution.py:24
  27.7 21.0 %collective-permute-start.2 = (bf16[896,256]{1,0:T(8,128)(2,1)S(1)}, bf16[896,256]{1,0:T(8,128)(2,1)S(1)}, u32[]{:S(2)}, u32[]{:S(2)}) collective-permute-start(bf16[896,256]{1,0:T(8,128)(2,1)S(1)} %collective-permute-done.1.refs_2_), channel_id=1, source_target_pairs={{0,8},{1,9},{2,10},{3,11},{4,0},{5,1},{6,2},{7,3},{8,16},{9,17},{1... | collective-permute-start | bytes 1376264 | tf_op jit(solution)/shard_map/ppermute | solution.py:24
  28.9 21.0 %collective-permute-start.6 = (bf16[896,256]{1,0:T(8,128)(2,1)S(1)}, bf16[896,256]{1,0:T(8,128)(2,1)S(1)}, u32[]{:S(2)}, u32[]{:S(2)}) collective-permute-start(bf16[896,256]{1,0:T(8,128)(2,1)S(1)} %collective-permute-done.5.refs_3_), channel_id=1, source_target_pairs={{8,0},{9,1},{10,2},{11,3},{0,4},{1,5},{2,6},{3,7},{16,8},{17,9},{1... | collective-permute-start | bytes 1376264 | tf_op jit(solution)/shard_map/ppermute | solution.py:24
  48.7 11.3 %collective-permute-start.3 = (bf16[448,256]{1,0:T(8,128)(2,1)S(1)}, bf16[448,256]{1,0:T(8,128)(2,1)S(1)}, u32[]{:S(2)}, u32[]{:S(2)}) collective-permute-start(bf16[448,256]{1,0:T(8,128)(2,1)S(1)} %slice.76), channel_id=1, source_target_pairs={{0,8},{1,9},{2,10},{3,11},{4,0},{5,1},{6,2},{7,3},{8,16},{9,17},{1... | collective-permute-start | bytes 688136 | tf_op jit(solution)/shard_map/ppermute | solution.py:24
  74.1 15.0 %collective-permute-start.11 = (f32[896,256]{1,0:T(8,128)S(1)}, f32[896,256]{1,0:T(8,128)S(1)}, u32[]{:S(2)}, u32[]{:S(2)}) collective-permute-start(f32[896,256]{1,0:T(8,128)S(1)} %copy-done.1), channel_id=1, source_target_pairs={{0,0},{4,1},{8,2},{12,3},{16,4},{20,5},{24,6},{28,7},{1,8},{5,9},{... | collective-permute-start | bytes 2752520 | tf_op jit(solution)/shard_map/ppermute | solution.py:24
  77.6 31.9 %collective-permute-start.10 = (bf16[896,256]{1,0:T(8,128)(2,1)S(1)}, bf16[896,256]{1,0:T(8,128)(2,1)S(1)}, u32[]{:S(2)}, u32[]{:S(2)}) collective-permute-start(bf16[896,256]{1,0:T(8,128)(2,1)S(1)} %get-tuple-element.62), channel_id=1, source_target_pairs={{0,2},{1,3},{2,0},{3,1},{4,6},{5,7},{6,4},{7,5},{8,10},{9,11},{10,... | collective-permute-start | bytes 1376264 | tf_op jit(solution)/shard_map/ppermute | solution.py:24
  124.5 13.2 %collective-permute-start.14 = (f32[96,256]{1,0:T(8,128)S(1)}, f32[96,256]{1,0:T(8,128)S(1)}, u32[]{:S(2)}, u32[]{:S(2)}) collective-permute-start(f32[96,256]{1,0:T(8,128)S(1)} %constant_dynamic-slice_fusion.12), channel_id=1, source_target_pairs={{0,4},{1,5},{2,6},{3,7},{4,0},{5,1},{6,2},{7,3},{8,12},{9,13},{10,... | collective-permute-start | bytes 294920 | tf_op jit(solution)/shard_map/ppermute | solution.py:24
  162.0 11.9 %collective-permute-start.21 = (f32[384,256]{1,0:T(8,128)}, f32[384,256]{1,0:T(8,128)}, u32[]{:S(2)}, u32[]{:S(2)}) collective-permute-start(f32[384,256]{1,0:T(8,128)} %pad_maximum_fusion.6), channel_id=1, source_target_pairs={{0,1},{1,0},{2,3},{3,2},{4,5},{5,4},{6,7},{7,6},{8,9},{9,8},{10,11... | collective-permute-start | bytes 1179656 | tf_op jit(solution)/shard_map/ppermute | solution.py:24
  170.8 63.8 %collective-permute-start.22 = (f32[896,256]{1,0:T(8,128)S(1)}, f32[896,256]{1,0:T(8,128)}, u32[]{:S(2)}, u32[]{:S(2)}) collective-permute-start(f32[896,256]{1,0:T(8,128)S(1)} %copy-done.3), channel_id=1, source_target_pairs={{0,0},{1,4},{2,8},{3,12},{4,16},{5,20},{6,24},{7,28},{8,1},{9,5},{... | collective-permute-start | bytes 2752520 | tf_op jit(solution)/shard_map/ppermute | solution.py:24
  237.5 12.2 %collective-permute-start.27 = (bf16[896,256]{1,0:T(8,128)(2,1)S(1)}, bf16[896,256]{1,0:T(8,128)(2,1)S(1)}, u32[]{:S(2)}, u32[]{:S(2)}) collective-permute-start(bf16[896,256]{1,0:T(8,128)(2,1)S(1)} %get-tuple-element.34.refs_1_), channel_id=1, source_target_pairs={{8,0},{9,1},{10,2},{11,3},{0,4},{1,5},{2,6},{3,7},{16,8},{17,9},{1... | collective-permute-start | bytes 1376264 | tf_op jit(solution)/shard_map/ppermute | solution.py:24
  247.6 11.4 %collective-permute-start.24 = (bf16[896,256]{1,0:T(8,128)(2,1)S(1)}, bf16[896,256]{1,0:T(8,128)(2,1)S(1)}, u32[]{:S(2)}, u32[]{:S(2)}) collective-permute-start(bf16[896,256]{1,0:T(8,128)(2,1)S(1)} %collective-permute-done.23.refs_2_), channel_id=1, source_target_pairs={{0,8},{1,9},{2,10},{3,11},{4,0},{5,1},{6,2},{7,3},{8,16},{9,17},{1... | collective-permute-start | bytes 1376264 | tf_op jit(solution)/shard_map/ppermute | solution.py:24
  249.8 11.4 %collective-permute-start.28 = (bf16[896,256]{1,0:T(8,128)(2,1)S(1)}, bf16[896,256]{1,0:T(8,128)(2,1)S(1)}, u32[]{:S(2)}, u32[]{:S(2)}) collective-permute-start(bf16[896,256]{1,0:T(8,128)(2,1)S(1)} %collective-permute-done.27.refs_3_), channel_id=1, source_target_pairs={{8,0},{9,1},{10,2},{11,3},{0,4},{1,5},{2,6},{3,7},{16,8},{17,9},{1... | collective-permute-start | bytes 1376264 | tf_op jit(solution)/shard_map/ppermute | solution.py:24
  258.9 22.4 %collective-permute-start.25 = (bf16[896,256]{1,0:T(8,128)(2,1)S(1)}, bf16[896,256]{1,0:T(8,128)(2,1)S(1)}, u32[]{:S(2)}, u32[]{:S(2)}) collective-permute-start(bf16[896,256]{1,0:T(8,128)(2,1)S(1)} %collective-permute-done.24.refs_2_), channel_id=1, source_target_pairs={{0,8},{1,9},{2,10},{3,11},{4,0},{5,1},{6,2},{7,3},{8,16},{9,17},{1... | collective-permute-start | bytes 1376264 | tf_op jit(solution)/shard_map/ppermute | solution.py:24
  261.1 21.0 %collective-permute-start.29 = (bf16[896,256]{1,0:T(8,128)(2,1)S(1)}, bf16[896,256]{1,0:T(8,128)(2,1)S(1)}, u32[]{:S(2)}, u32[]{:S(2)}) collective-permute-start(bf16[896,256]{1,0:T(8,128)(2,1)S(1)} %collective-permute-done.28.refs_3_), channel_id=1, source_target_pairs={{8,0},{9,1},{10,2},{11,3},{0,4},{1,5},{2,6},{3,7},{16,8},{17,9},{1... | collective-permute-start | bytes 1376264 | tf_op jit(solution)/shard_map/ppermute | solution.py:24
  281.3 11.7 %collective-permute-start.26 = (bf16[448,256]{1,0:T(8,128)(2,1)S(1)}, bf16[448,256]{1,0:T(8,128)(2,1)S(1)}, u32[]{:S(2)}, u32[]{:S(2)}) collective-permute-start(bf16[448,256]{1,0:T(8,128)(2,1)S(1)} %slice.83), channel_id=1, source_target_pairs={{0,8},{1,9},{2,10},{3,11},{4,0},{5,1},{6,2},{7,3},{8,16},{9,17},{1... | collective-permute-start | bytes 688136 | tf_op jit(solution)/shard_map/ppermute | solution.py:24
  282.2 10.9 %collective-permute-start.30 = (bf16[448,256]{1,0:T(8,128)(2,1)S(1)}, bf16[448,256]{1,0:T(8,128)(2,1)S(1)}, u32[]{:S(2)}, u32[]{:S(2)}) collective-permute-start(bf16[448,256]{1,0:T(8,128)(2,1)S(1)} %slice.84), channel_id=1, source_target_pairs={{8,0},{9,1},{10,2},{11,3},{0,4},{1,5},{2,6},{3,7},{16,8},{17,9},{1... | collective-permute-start | bytes 688136 | tf_op jit(solution)/shard_map/ppermute | solution.py:24
  305.5 12.0 %collective-permute-start.33 = (bf16[896,256]{1,0:T(8,128)(2,1)S(1)}, bf16[896,256]{1,0:T(8,128)(2,1)S(1)}, u32[]{:S(2)}, u32[]{:S(2)}) collective-permute-start(bf16[896,256]{1,0:T(8,128)(2,1)S(1)} %get-tuple-element.60), channel_id=1, source_target_pairs={{0,2},{1,3},{2,0},{3,1},{4,6},{5,7},{6,4},{7,5},{8,10},{9,11},{10,... | collective-permute-start | bytes 1376264 | tf_op jit(solution)/shard_map/ppermute | solution.py:24
  354.2 11.2 %collective-permute-start.43 = (f32[384,256]{1,0:T(8,128)S(1)}, f32[384,256]{1,0:T(8,128)S(1)}, u32[]{:S(2)}, u32[]{:S(2)}) collective-permute-start(f32[384,256]{1,0:T(8,128)S(1)} %pad_maximum_fusion.7), channel_id=1, source_target_pairs={{0,1},{1,0},{2,3},{3,2},{4,5},{5,4},{6,7},{7,6},{8,9},{9,8},{10,11... | collective-permute-start | bytes 1179656 | tf_op jit(solution)/shard_map/ppermute | solution.py:24
  363.5 63.5 %collective-permute-start.44 = (f32[896,256]{1,0:T(8,128)S(1)}, f32[896,256]{1,0:T(8,128)S(1)}, u32[]{:S(2)}, u32[]{:S(2)}) collective-permute-start(f32[896,256]{1,0:T(8,128)S(1)} %get-tuple-element.41.image), channel_id=1, source_target_pairs={{0,0},{1,4},{2,8},{3,12},{4,16},{5,20},{6,24},{7,28},{8,1},{9,5},{... | collective-permute-start | bytes 2752520 | tf_op jit(solution)/shard_map/ppermute | solution.py:24
  429.7 12.2 %collective-permute-start.49 = (bf16[896,256]{1,0:T(8,128)(2,1)S(1)}, bf16[896,256]{1,0:T(8,128)(2,1)S(1)}, u32[]{:S(2)}, u32[]{:S(2)}) collective-permute-start(bf16[896,256]{1,0:T(8,128)(2,1)S(1)} %get-tuple-element.44.refs_1_), channel_id=1, source_target_pairs={{8,0},{9,1},{10,2},{11,3},{0,4},{1,5},{2,6},{3,7},{16,8},{17,9},{1... | collective-permute-start | bytes 1376264 | tf_op jit(solution)/shard_map/ppermute | solution.py:24
  439.7 11.3 %collective-permute-start.46 = (bf16[896,256]{1,0:T(8,128)(2,1)S(1)}, bf16[896,256]{1,0:T(8,128)(2,1)S(1)}, u32[]{:S(2)}, u32[]{:S(2)}) collective-permute-start(bf16[896,256]{1,0:T(8,128)(2,1)S(1)} %collective-permute-done.45.refs_2_), channel_id=1, source_target_pairs={{0,8},{1,9},{2,10},{3,11},{4,0},{5,1},{6,2},{7,3},{8,16},{9,17},{1... | collective-permute-start | bytes 1376264 | tf_op jit(solution)/shard_map/ppermute | solution.py:24
  441.9 11.3 %collective-permute-start.50 = (bf16[896,256]{1,0:T(8,128)(2,1)S(1)}, bf16[896,256]{1,0:T(8,128)(2,1)S(1)}, u32[]{:S(2)}, u32[]{:S(2)}) collective-permute-start(bf16[896,256]{1,0:T(8,128)(2,1)S(1)} %collective-permute-done.49.refs_3_), channel_id=1, source_target_pairs={{8,0},{9,1},{10,2},{11,3},{0,4},{1,5},{2,6},{3,7},{16,8},{17,9},{1... | collective-permute-start | bytes 1376264 | tf_op jit(solution)/shard_map/ppermute | solution.py:24
  451.0 22.8 %collective-permute-start.47 = (bf16[896,256]{1,0:T(8,128)(2,1)S(1)}, bf16[896,256]{1,0:T(8,128)(2,1)S(1)}, u32[]{:S(2)}, u32[]{:S(2)}) collective-permute-start(bf16[896,256]{1,0:T(8,128)(2,1)S(1)} %collective-permute-done.46.refs_2_), channel_id=1, source_target_pairs={{0,8},{1,9},{2,10},{3,11},{4,0},{5,1},{6,2},{7,3},{8,16},{9,17},{1... | collective-permute-start | bytes 1376264 | tf_op jit(solution)/shard_map/ppermute | solution.py:24
  453.2 21.0 %collective-permute-start.51 = (bf16[896,256]{1,0:T(8,128)(2,1)S(1)}, bf16[896,256]{1,0:T(8,128)(2,1)S(1)}, u32[]{:S(2)}, u32[]{:S(2)}) collective-permute-start(bf16[896,256]{1,0:T(8,128)(2,1)S(1)} %collective-permute-done.50.refs_3_), channel_id=1, source_target_pairs={{8,0},{9,1},{10,2},{11,3},{0,4},{1,5},{2,6},{3,7},{16,8},{17,9},{1... | collective-permute-start | bytes 1376264 | tf_op jit(solution)/shard_map/ppermute | solution.py:24
  473.9 11.3 %collective-permute-start.48 = (bf16[448,256]{1,0:T(8,128)(2,1)S(1)}, bf16[448,256]{1,0:T(8,128)(2,1)S(1)}, u32[]{:S(2)}, u32[]{:S(2)}) collective-permute-start(bf16[448,256]{1,0:T(8,128)(2,1)S(1)} %slice.89), channel_id=1, source_target_pairs={{0,8},{1,9},{2,10},{3,11},{4,0},{5,1},{6,2},{7,3},{8,16},{9,17},{1... | collective-permute-start | bytes 688136 | tf_op jit(solution)/shard_map/ppermute | solution.py:24
  474.3 10.9 %collective-permute-start.52 = (bf16[448,256]{1,0:T(8,128)(2,1)S(1)}, bf16[448,256]{1,0:T(8,128)(2,1)S(1)}, u32[]{:S(2)}, u32[]{:S(2)}) collective-permute-start(bf16[448,256]{1,0:T(8,128)(2,1)S(1)} %slice.90), channel_id=1, source_target_pairs={{8,0},{9,1},{10,2},{11,3},{0,4},{1,5},{2,6},{3,7},{16,8},{17,9},{1... | collective-permute-start | bytes 688136 | tf_op jit(solution)/shard_map/ppermute | solution.py:24
  497.5 12.0 %collective-permute-start.55 = (bf16[896,256]{1,0:T(8,128)(2,1)S(1)}, bf16[896,256]{1,0:T(8,128)(2,1)S(1)}, u32[]{:S(2)}, u32[]{:S(2)}) collective-permute-start(bf16[896,256]{1,0:T(8,128)(2,1)S(1)} %get-tuple-element.58), channel_id=1, source_target_pairs={{0,2},{1,3},{2,0},{3,1},{4,6},{5,7},{6,4},{7,5},{8,10},{9,11},{10,... | collective-permute-start | bytes 1376264 | tf_op jit(solution)/shard_map/ppermute | solution.py:24
  546.2 13.3 %collective-permute-start.65 = (f32[384,256]{1,0:T(8,128)S(1)}, f32[384,256]{1,0:T(8,128)S(1)}, u32[]{:S(2)}, u32[]{:S(2)}) collective-permute-start(f32[384,256]{1,0:T(8,128)S(1)} %pad_maximum_fusion.8), channel_id=1, source_target_pairs={{0,1},{1,0},{2,3},{3,2},{4,5},{5,4},{6,7},{7,6},{8,9},{9,8},{10,11... | collective-permute-start | bytes 1179656 | tf_op jit(solution)/shard_map/ppermute | solution.py:24
  557.4 63.3 %collective-permute-start.66 = (f32[896,256]{1,0:T(8,128)S(1)}, f32[896,256]{1,0:T(8,128)}, u32[]{:S(2)}, u32[]{:S(2)}) collective-permute-start(f32[896,256]{1,0:T(8,128)S(1)} %get-tuple-element.51), channel_id=1, source_target_pairs={{0,0},{1,4},{2,8},{3,12},{4,16},{5,20},{6,24},{7,28},{8,1},{9,5},{... | collective-permute-start | bytes 2752520 | tf_op jit(solution)/shard_map/ppermute | solution.py:24
  (45 other events, 258.9 us)

commit v2 on v1

v2 whole, which is shorter than its diff:
```python
import functools

import jax
import jax.numpy as jnp
import numpy as np
from jax import lax
from jax.experimental import pallas as pl
from jax.experimental.pallas import tpu as pltpu
from jax.sharding import PartitionSpec as P

ITERS = 3
AXES = ("row", "col")
HIGHEST = lax.Precision.HIGHEST
VMEM_LIMIT = 48 * 1024 * 1024
DONE = 3e-8
MAX_SQUARINGS = 48


def dot(left, right):
    return jnp.dot(left, right, precision=HIGHEST, preferred_element_type=jnp.float32)


def send(block, pairs):
    return lax.ppermute(block, AXES, pairs)


def vmem_params(**extra):
    return pltpu.CompilerParams(vmem_limit_bytes=VMEM_LIMIT, **extra)


def bits_of(size, first_stride):
    assert size & (size - 1) == 0
    return [first_stride << b for b in range(size.bit_length() - 1)]


def ring_order(rows):
    fast = 1 << ((rows.bit_length() - 1) // 2)
    slow = rows // fast
    if fast == 1 or slow == 1:
        return list(range(rows))
    cycle = [s * fast for s in range(slow)]
    for s in reversed(range(slow)):
        lane = range(1, fast) if (slow - 1 - s) % 2 == 0 else reversed(range(1, fast))
        cycle += [s * fast + f for f in lane]
    return cycle


def index_table(order, cols):
    rows = len(order)
    place = {r: i for i, r in enumerate(order)}
    shifts = [0] + [s for d in range(1, rows // 2) for s in (-d, d)] + [rows // 2]
    return np.array(
        [
            [c ^ j for j in range(cols)] + [order[(place[r] + s) % rows] for s in shifts]
            for r in range(rows)
            for c in range(cols)
        ],
        np.int32,
    )


def chunk_kernel(blocks, has_base, index_ref, *refs):
    covs, parts = refs[:blocks], refs[blocks : 2 * blocks]
    out = refs[-1]
    total = refs[2 * blocks][...] if has_base else None
    for cov, part in zip(covs, parts):
        term = jnp.dot(cov[...], part[...], preferred_element_type=jnp.float32)
        total = term if total is None else total + term
    out[...] = total


def add_chunks(covariance, index, cols, first_owner, parts, base, begin, count):
    blocks = len(parts)
    depth, edits = parts[0].shape
    height = covariance.shape[0] // cols
    has_base = base is not None

    def cov_spec(t):
        return pl.BlockSpec((height, depth), lambda i, ix: (ix[begin + i], ix[cols + first_owner + t]))

    part_specs = [pl.BlockSpec((depth, edits), lambda i, ix: (0, 0)) for _ in parts]
    base_spec = [pl.BlockSpec((height, edits), lambda i, ix: (begin + i, 0))] if has_base else []
    operands = [covariance] * blocks + list(parts) + ([base] if has_base else [])
    whole = has_base and count == cols
    return pl.pallas_call(
        functools.partial(chunk_kernel, blocks, has_base),
        grid_spec=pltpu.PrefetchScalarGridSpec(
            num_scalar_prefetch=1,
            grid=(count,),
            in_specs=[cov_spec(t) for t in range(blocks)] + part_specs + base_spec,
            out_specs=pl.BlockSpec((height, edits), lambda i, ix: (i, 0)),
        ),
        out_shape=jax.ShapeDtypeStruct((count * height, edits), jnp.float32),
        input_output_aliases={1 + 2 * blocks: 0} if whole else {},
        compiler_params=vmem_params(),
        cost_estimate=pl.CostEstimate(
            flops=2 * count * height * depth * blocks * edits,
            bytes_accessed=2 * count * height * depth * blocks,
            transcendentals=0,
        ),
    )(index, *operands)


def partial_image(covariance, lowered, order, index, cols, aside):
    rows = len(order)
    depth = lowered.shape[0]
    quarter = covariance.shape[0] // cols
    if depth % 128 or depth % 32 or quarter % 16 or rows % 2:
        whole = lax.all_gather(lowered, "row", axis=0, tiled=True)
        product = jnp.dot(covariance, whole, preferred_element_type=jnp.float32)
        swapped = product.reshape(cols, quarter, -1)[index[:cols]]
        return [swapped[j] for j in range(cols)], aside
    following = {order[i]: order[(i + 1) % rows] for i in range(rows)}
    forward = [(r * cols + c, following[r] * cols + c) for r in range(rows) for c in range(cols)]
    backward = [(b, a) for a, b in forward]
    half = depth // 2
    ahead = behind = lowered
    held, owner, total = [lowered], 0, None
    for step in range(1, rows // 2 + 1):
        if step < rows // 2:
            behind, ahead = send(behind, forward), send(ahead, backward)
            arrived = [behind, ahead]
        else:
            arrived = [jnp.concatenate([send(behind[:half], forward), send(ahead[half:], backward)])]
        total = add_chunks(covariance, index, cols, owner, held, total, 0, cols)
        owner += len(held)
        if step < rows // 2:
            if step == 2:
                total, aside = lax.optimization_barrier((total, aside))
            total, behind, ahead = lax.optimization_barrier((total, behind, ahead))
            arrived = [behind, ahead]
        held = arrived
    upper = add_chunks(covariance, index, cols, owner, held, total, cols // 2, cols // 2)
    lower = add_chunks(covariance, index, cols, owner, held, total, 0, cols // 2)
    return [part[j * quarter : (j + 1) * quarter] for part in (lower, upper) for j in range(cols // 2)], aside


def exchange_sum(pieces, rows):
    cols = len(pieces)
    pieces = dict(enumerate(pieces))
    strides = bits_of(cols, 1)
    for bit in strides:
        pairs = [(i, i ^ bit) for i in range(rows * cols)]
        got = {}
        for j in sorted((j for j in pieces if j & bit), reverse=True):
            block = pieces[j].astype(jnp.bfloat16) if bit > 1 else pieces[j]
            got[j ^ bit] = send(block, pairs)
        if bit == strides[-1]:
            return pieces[0], got[0]
        pieces = {j: pieces[j] + got[j].astype(jnp.float32) for j in got}


def gram_kernel(first, own, got, residual, *refs):
    direction = None if first else refs[0]
    image, grams = refs[-2:]
    image[...] = (own[...] + got[...].astype(jnp.float32)).astype(jnp.bfloat16)
    value = image[...].astype(jnp.float32)
    order = value.shape[1]
    flipped = value.T
    grams[0:order] = dot(flipped, value)
    grams[order : 2 * order] = dot(flipped, residual[...])
    if first:
        grams[2 * order :] = dot(residual[...].T, residual[...])
    else:
        grams[2 * order :] = dot(flipped, direction[...])


def local_grams(own, got, residual, direction, first):
    rows, edits = own.shape
    operands = [own, got, residual] + ([] if first else [direction])
    return pl.pallas_call(
        functools.partial(gram_kernel, first),
        out_shape=[
            jax.ShapeDtypeStruct((rows, edits), jnp.bfloat16),
            jax.ShapeDtypeStruct((3 * edits, edits), jnp.float32),
        ],
        compiler_params=vmem_params(),
        cost_estimate=pl.CostEstimate(
            flops=36 * rows * edits * edits, bytes_accessed=16 * rows * edits, transcendentals=0
        ),
    )(*operands)


def partners(total, stride, size, step):
    return [(i, i + (((i // stride) % size ^ step) - (i // stride) % size) * stride) for i in range(total)]


def sum_all(block, rows, cols, rider, hops):
    total = rows * cols
    me = lax.axis_index("row") * cols + lax.axis_index("col")
    plane = cols // 2 * min(2, rows)
    scatter = [(1, 2), (2, plane)]
    exchange = [(stride, 2) for stride in bits_of(total // (2 * plane), 2 * plane)]
    for stride, size in scatter:
        digit = (me // stride) % size
        piece = block.shape[0] // size
        got = [
            send(lax.dynamic_slice_in_dim(block, (digit ^ step) * piece, piece, 0), partners(total, stride, size, step))
            for step in range(1, size)
        ]
        block = lax.dynamic_slice_in_dim(block, digit * piece, piece, 0)
        for term in got:
            block = block + term
    block, rider = lax.optimization_barrier((block, rider))
    rider = send(rider, hops[0])
    for stride, _ in exchange:
        block = block + send(block, partners(total, stride, 2, 1))
    block, rider = lax.optimization_barrier((block, rider))
    rider = send(rider, hops[1])
    for stride, size in reversed(scatter):
        digit = (me // stride) % size
        piece = block.shape[0]
        whole = jnp.zeros((size * piece,) + block.shape[1:], block.dtype)
        for step in range(size):
            part = send(block, partners(total, stride, size, step)) if step else block
            whole = lax.dynamic_update_slice_in_dim(whole, part, (digit ^ step) * piece, 0)
        block = whole
    return block, rider


def squared_norm(matrix):
    return jnp.sum(matrix * matrix)


def power_solve(matrix, rhs, scale_ref, error_ref, value_ref):
    order = matrix.shape[0]
    row = lax.broadcasted_iota(jnp.int32, (order, order), 0)
    col = lax.broadcasted_iota(jnp.int32, (order, order), 1)
    eye = jnp.where(row == col, 1.0, 0.0).astype(jnp.float32)
    diagonal = matrix * eye
    across = lax.rsqrt(jnp.sum(diagonal, axis=0, keepdims=True))
    scale_ref[...] = lax.rsqrt(jnp.sum(diagonal, axis=1, keepdims=True))
    unit = matrix * across * scale_ref[...]
    error = eye - unit
    square = dot(error, error)
    size = squared_norm(square)
    safe = size < 0.9
    start = scale_ref[...] * (eye if rhs is None else rhs)

    @pl.when(safe)
    def _():
        value_ref[...] = start + dot(error, start)
        error_ref[...] = square

    @pl.when(jnp.logical_not(safe))
    def _():
        factor = 1.0 / jnp.max(jnp.sum(jnp.abs(unit), axis=1))
        value_ref[...] = factor * start
        error_ref[...] = eye - factor * unit

    def step(state):
        count, _ = state
        error = error_ref[...]
        value_ref[...] += dot(error, value_ref[...])
        error_ref[...] = dot(error, error)
        return count + 1, squared_norm(error)

    lax.while_loop(lambda s: (s[0] < MAX_SQUARINGS) & (s[1] > DONE), step, (0, jnp.float32(1.0)))
    return scale_ref[...] * value_ref[...]


def solve_kernel(first, grams, *refs):
    alpha, beta, norm_out, scale, error, value = refs[-6:]
    order = alpha.shape[0]
    square = grams[0:order]
    cross = grams[order : 2 * order]
    norm = grams[2 * order :] if first else refs[0][...]
    curvature = cross if first else grams[2 * order :]
    curvature = 0.5 * (curvature + curvature.T)
    step = power_solve(curvature, norm, scale, error, value)
    alpha[...] = step
    change = dot(step.T, dot(square, step) - 2.0 * cross)
    after = norm + 0.5 * (change + change.T)
    norm_out[...] = after
    beta[...] = power_solve(norm, after, scale, error, value) if first else dot(refs[1][...], after)


def small_scratch(edits):
    return [
        pltpu.VMEM((edits, 1), jnp.float32),
        pltpu.VMEM((edits, edits), jnp.float32),
        pltpu.VMEM((edits, edits), jnp.float32),
    ]


def solve_small(grams, norm, inverse):
    edits = grams.shape[1]
    square = jax.ShapeDtypeStruct((edits, edits), jnp.float32)
    return pl.pallas_call(
        functools.partial(solve_kernel, norm is None),
        out_shape=[square, square, square],
        scratch_shapes=small_scratch(edits),
        compiler_params=vmem_params(),
        cost_estimate=pl.CostEstimate(
            flops=100 * edits * edits * edits, bytes_accessed=32 * edits * edits, transcendentals=0
        ),
    )(grams, *([] if norm is None else [norm, inverse]))


def inverse_kernel(matrix, out, scale, error, value):
    out[...] = power_solve(matrix[...], None, scale, error, value)


def inverse_small(matrix):
    edits = matrix.shape[0]
    return pl.pallas_call(
        inverse_kernel,
        out_shape=jax.ShapeDtypeStruct((edits, edits), jnp.float32),
        scratch_shapes=small_scratch(edits),
        compiler_params=vmem_params(),
        cost_estimate=pl.CostEstimate(
            flops=100 * edits * edits * edits, bytes_accessed=8 * edits * edits, transcendentals=0
        ),
    )(matrix)


def update_kernel(residual, direction, image, alpha, beta, residual_out, direction_out, lowered_out):
    after = residual[...] - dot(image[...].astype(jnp.float32), alpha[...])
    residual_out[...] = after
    following = after + dot(direction[...], beta[...])
    direction_out[...] = following
    lowered_out[...] = following.astype(jnp.bfloat16)


def update(residual, direction, image, alpha, beta):
    rows, edits = residual.shape
    full = jax.ShapeDtypeStruct((rows, edits), jnp.float32)
    return pl.pallas_call(
        update_kernel,
        out_shape=[full, full, jax.ShapeDtypeStruct((rows, edits), jnp.bfloat16)],
        compiler_params=vmem_params(),
        cost_estimate=pl.CostEstimate(
            flops=24 * rows * edits * edits, bytes_accessed=22 * rows * edits, transcendentals=0
        ),
    )(residual, direction, image, alpha, beta)


def advance_kernel(iterate, direction, alpha, out):
    out[...] = iterate[...] + dot(direction[...], alpha[...])


def start_kernel(direction, alpha, out):
    out[...] = dot(direction[...], alpha[...])


def advance(iterate, direction, alpha):
    rows, edits = direction.shape
    return pl.pallas_call(
        start_kernel if iterate is None else advance_kernel,
        out_shape=jax.ShapeDtypeStruct((rows, edits), jnp.float32),
        compiler_params=vmem_params(),
        cost_estimate=pl.CostEstimate(
            flops=12 * rows * edits * edits, bytes_accessed=12 * rows * edits, transcendentals=0
        ),
    )(*([] if iterate is None else [iterate]), direction, alpha)


def body(rows, cols, covariance, right_side):
    total = rows * cols
    order = ring_order(rows)
    me = lax.axis_index("row") * cols + lax.axis_index("col")
    table = index_table(order, cols)
    index = lax.dynamic_index_in_dim(jnp.asarray(table), me, 0, keepdims=False)
    to_outer = {k: (k % rows) * cols + k // rows for k in range(total)}
    swap = {k: k ^ (cols + 1) if (k // cols ^ k) & 1 else k for k in range(total)}
    hops = [list(swap.items()), [(swap[k], to_outer[k]) for k in range(total)]]
    residual = direction = right_side
    inner_residual = inner_direction = send(right_side, [(b, a) for a, b in to_outer.items()])
    lowered = right_side.astype(jnp.bfloat16)
    iterate = norm = inverse = alpha = earlier = None
    for iteration in range(ITERS):
        first, last = iteration == 0, iteration == ITERS - 1
        aside = () if first else (inverse_small(norm), advance(iterate, earlier, alpha))
        pieces, aside = partial_image(covariance, lowered, order, index, cols, aside)
        if not first:
            inverse, iterate = aside
        own, got = exchange_sum(pieces, rows)
        inner_image, grams = local_grams(own, got, inner_residual, inner_direction, first)
        grams, image = sum_all(grams, rows, cols, inner_image, hops)
        alpha, beta, norm = solve_small(grams, norm, inverse)
        earlier = direction
        residual, direction, lowered = update(residual, direction, image, alpha, beta)
        if not last:
            inner_residual, inner_direction, _ = update(
                inner_residual, inner_direction, inner_image, alpha, beta
            )
    return (advance(iterate, earlier, alpha), residual, direction)


def solution(mesh):
    place = P(("col", "row"), None)
    return jax.shard_map(
        functools.partial(body, mesh.shape["row"], mesh.shape["col"]),
        mesh=mesh,
        in_specs=(P("row", "col"), place),
        out_specs=(place, place, place),
        check_vma=False,
    )
```

time: 635 us -> 437 us (0.69)
  waiting for transfers between devices: 274 us -> 122 us
  Pallas kernels: 212 us -> 194 us
  other arithmetic: 14.9 us -> 4.23 us
  starting transfers between devices: 106 us -> 98.8 us
    ppermute x67 -> x70, waiting for transfers between devices: 274 us -> 122 us  [send(): return lax.ppermute(block, AXES, pairs)]
    pallas_call x15 -> x18, Pallas kernels: 132 us -> 108 us  [add_chunks(): pl.pallas_call(functools.partial(chunk_kernel, blocks, has_base), grid_sp...]
    ppermute x67 -> x70, starting transfers between devices: 106 us -> 98.8 us  [send(): return lax.ppermute(block, AXES, pairs)]
    pallas_call x3 -> x8, Pallas kernels: 57.1 us -> 63.6 us  [the longest x3 41.7 us: solve_small(): pl.pallas_call(functools.partial(solve_kernel, norm is None), out_shape=[...]
  transfers between devices with their start and end apart: 67 -> 70, of which waited for: 42 -> 42; matrix products, arithmetic and copies ran while one was open for 3% -> 1% of each run, Pallas kernels for 27% -> 39%
where the time goes in v2:
time: 437 us; the launch traced here: 429 us
  Pallas kernels  194 us (44%)
  waiting for transfers between devices  122 us (28%)
  starting transfers between devices  98.8 us (23%)
  local copies, waits for them, and re-layouts  7.66 us (2%)
    ppermute x70, waiting for transfers between devices, send(): return lax.ppermute(block, AXES, pairs)  122 us
    pallas_call x18, Pallas kernels, add_chunks(): pl.pallas_call(functools.partial(chunk_kernel, blocks, has_base), grid_sp...  108 us
    ppermute x70, starting transfers between devices, send(): return lax.ppermute(block, AXES, pairs)  98.8 us
    pallas_call x3, Pallas kernels, solve_small(): pl.pallas_call(functools.partial(solve_kernel, norm is None), out_shape=[...  41.7 us
    pallas_call x2, Pallas kernels, inverse_small(): pl.pallas_call(inverse_kernel, out_shape=jax.ShapeDtypeStruct((edits, edi...  18.4 us
    pallas_call x5, Pallas kernels, update(): pl.pallas_call(update_kernel, out_shape=[full, full, jax.ShapeDtypeStruct...  13 us
    pallas_call x3, Pallas kernels, local_grams(): pl.pallas_call(functools.partial(gram_kernel, first), out_shape=[jax.Shap...  9.66 us
  transfers between devices with their start and end apart: 70, of which 42 were waited for; matrix products, arithmetic and copies ran while one was open for 1% of the time, Pallas kernels for 39%

profile of v2, /device:TPU:1, one launch (start us, length us, event | category | flops | bytes accessed | tf_op | source)
XLA Modules:
  0.0 429.0 jit_solution(5119416195888229863)
XLA Ops:
  4.7 5.5 %shard_map.58.refs_4_ = f32[3584,256]{1,0:T(8,128)S(1)} custom-call(s32[12]{0:T(128)S(1)} %fusion.3.index_ref, bf16[3584,7168]{1,0:T(8,128)(2,1)} %refs_0_.35, bf16[896,256]{1,0:T(8,128)(2,1)S(1)} %convert_element_type.12.refs_1_), custom_call_target="tpu_custom_call" | custom-call | flops 1644167168 | bytes 6422528 | tf_op jit(solution)/shard_map/pallas_call | solution.py:85
  10.2 4.0 collective-permute-done.refs_2_
  16.6 8.0 %shard_map.59.refs_4_ = f32[3584,256]{1,0:T(8,128)S(1)} custom-call(s32[12]{0:T(128)S(1)} %fusion.3.index_ref, bf16[3584,7168]{1,0:T(8,128)(2,1)} %refs_0_.35, bf16[3584,7168]{1,0:T(8,128)(2,1)} %refs_0_.35, bf16[896,256]{1,0:T(8,128)(2,1)S(1)} %collective-permute-done.refs_2_, ...), custom_call_target="tpu_custom_call", output_to_operand_aliasing={{}: (5, {})} | custom-call | flops 3288334336 | bytes 12845056 | tf_op jit(solution)/shard_map/pallas_call | solution.py:85
  27.7 8.0 %shard_map.60.refs_4_ = f32[3584,256]{1,0:T(8,128)S(1)} custom-call(s32[12]{0:T(128)S(1)} %fusion.3.index_ref, bf16[3584,7168]{1,0:T(8,128)(2,1)} %refs_0_.35, bf16[3584,7168]{1,0:T(8,128)(2,1)} %refs_0_.35, bf16[896,256]{1,0:T(8,128)(2,1)S(1)} %collective-permute-done.2.refs_2_, ...), custom_call_target="tpu_custom_call", output_to_operand_aliasing={{}: (5, {})} | custom-call | flops 3288334336 | bytes 12845056 | tf_op jit(solution)/shard_map/pallas_call | solution.py:85
  37.8 8.0 %shard_map.61.refs_2_ = f32[3584,256]{1,0:T(8,128)S(1)} custom-call(s32[12]{0:T(128)S(1)} %fusion.3.index_ref, bf16[3584,7168]{1,0:T(8,128)(2,1)} %refs_0_.35, bf16[3584,7168]{1,0:T(8,128)(2,1)} %refs_0_.35, bf16[896,256]{1,0:T(8,128)(2,1)S(1)} %collective-permute-done.4.refs_2_, ...), custom_call_target="tpu_custom_call", output_to_operand_aliasing={{}: (5, {})} | custom-call | flops 3288334336 | bytes 12845056 | tf_op jit(solution)/shard_map/pallas_call | solution.py:85
  49.3 4.9 %collective-permute-start.9 = (f32[896,256]{1,0:T(8,128)S(1)}, f32[896,256]{1,0:T(8,128)S(1)}, u32[]{:S(2)}, u32[]{:S(2)}) collective-permute-start(f32[896,256]{1,0:T(8,128)S(1)} %slice.75), channel_id=1, source_target_pairs={{0,1},{1,0},{2,3},{3,2},{4,5},{5,4},{6,7},{7,6},{8,9},{9,8},{10,11... | collective-permute-start | bytes 2752520 | tf_op jit(solution)/shard_map/ppermute | solution.py:24
  65.7 7.8 %collective-permute-done.11.residual.direction = f32[896,256]{1,0:T(8,128)} collective-permute-done((f32[896,256]{1,0:T(8,128)S(1)}, f32[896,256]{1,0:T(8,128)}, u32[]{:S(2)}, u32[]{:S(2)}) %collective-permute-start.11) | collective-permute-done | bytes 917536 | tf_op jit(solution)/shard_map/ppermute | solution.py:24
  73.5 20.1 %collective-permute-done.10.got = bf16[896,256]{1,0:T(8,128)(2,1)S(1)} collective-permute-done((bf16[896,256]{1,0:T(8,128)(2,1)}, bf16[896,256]{1,0:T(8,128)(2,1)S(1)}, u32[]{:S(2)}, u32[]{:S(2)}) %collective-permute-start.10) | collective-permute-done | bytes 458784 | tf_op jit(solution)/shard_map/ppermute | solution.py:24
  95.4 4.0 shard_map.64
  103.5 8.2 %collective-permute-start.14 = (f32[96,256]{1,0:T(8,128)S(1)}, f32[96,256]{1,0:T(8,128)S(1)}, u32[]{:S(2)}, u32[]{:S(2)}) collective-permute-start(f32[96,256]{1,0:T(8,128)S(1)} %get-tuple-element.153), channel_id=1, source_target_pairs={{0,4},{1,5},{2,6},{3,7},{4,0},{5,1},{6,2},{7,3},{8,12},{9,13},{10,... | collective-permute-start | bytes 294920 | tf_op jit(solution)/shard_map/ppermute | solution.py:24
  126.8 5.4 %collective-permute-done.17 = f32[96,256]{1,0:T(8,128)S(1)} collective-permute-done((f32[96,256]{1,0:T(8,128)S(1)}, f32[96,256]{1,0:T(8,128)S(1)}, u32[]{:S(2)}, u32[]{:S(2)}) %collective-permute-start.17) | collective-permute-done | bytes 98336 | tf_op jit(solution)/shard_map/ppermute | solution.py:24
  143.6 18.7 %shard_map.65 = (f32[256,256]{1,0:T(8,128)S(1)}, f32[256,256]{1,0:T(8,128)S(1)}, f32[256,256]{1,0:T(8,128)S(1)}) custom-call(f32[768,256]{1,0:T(8,128)S(1)} %constant_dynamic-update-slice_fusion.18.grams), custom_call_target="tpu_custom_call" | custom-call | flops 1677721600 | bytes 2097152 | tf_op jit(solution)/shard_map/pallas_call | solution.py:289
  168.3 5.5 %shard_map.67.refs_4_ = f32[3584,256]{1,0:T(8,128)S(1)} custom-call(s32[12]{0:T(128)S(1)} %fusion.3.index_ref, bf16[3584,7168]{1,0:T(8,128)(2,1)} %refs_0_.35, bf16[896,256]{1,0:T(8,128)(2,1)S(1)} %get-tuple-element.93.refs_1_), custom_call_target="tpu_custom_call" | custom-call | flops 1644167168 | bytes 6422528 | tf_op jit(solution)/shard_map/pallas_call | solution.py:85
  178.3 8.9 %shard_map.69.refs_1_ = f32[256,256]{1,0:T(8,128)S(1)} custom-call(f32[256,256]{1,0:T(8,128)S(1)} %get-tuple-element.97.matrix.refs_0_), custom_call_target="tpu_custom_call" | custom-call | flops 1677721600 | bytes 524288 | tf_op jit(solution)/shard_map/pallas_call | solution.py:306
  187.2 8.0 %shard_map.68.refs_4_ = f32[3584,256]{1,0:T(8,128)S(1)} custom-call(s32[12]{0:T(128)S(1)} %fusion.3.index_ref, bf16[3584,7168]{1,0:T(8,128)(2,1)} %refs_0_.35, bf16[3584,7168]{1,0:T(8,128)(2,1)} %refs_0_.35, bf16[896,256]{1,0:T(8,128)(2,1)S(1)} %collective-permute-done.24.refs_2_, ...), custom_call_target="tpu_custom_call", output_to_operand_aliasing={{}: (5, {})} | custom-call | flops 3288334336 | bytes 12845056 | tf_op jit(solution)/shard_map/pallas_call | solution.py:85
  196.8 8.0 %shard_map.71.refs_4_ = f32[3584,256]{1,0:T(8,128)S(1)} custom-call(s32[12]{0:T(128)S(1)} %fusion.3.index_ref, bf16[3584,7168]{1,0:T(8,128)(2,1)} %refs_0_.35, bf16[3584,7168]{1,0:T(8,128)(2,1)} %refs_0_.35, bf16[896,256]{1,0:T(8,128)(2,1)S(1)} %collective-permute-done.26.refs_2_, ...), custom_call_target="tpu_custom_call", output_to_operand_aliasing={{}: (5, {})} | custom-call | flops 3288334336 | bytes 12845056 | tf_op jit(solution)/shard_map/pallas_call | solution.py:85
  208.1 8.0 %shard_map.72.refs_2_ = f32[3584,256]{1,0:T(8,128)S(1)} custom-call(s32[12]{0:T(128)S(1)} %fusion.3.index_ref, bf16[3584,7168]{1,0:T(8,128)(2,1)} %refs_0_.35, bf16[3584,7168]{1,0:T(8,128)(2,1)} %refs_0_.35, bf16[896,256]{1,0:T(8,128)(2,1)S(1)} %collective-permute-done.28.refs_2_, ...), custom_call_target="tpu_custom_call", output_to_operand_aliasing={{}: (5, {})} | custom-call | flops 3288334336 | bytes 12845056 | tf_op jit(solution)/shard_map/pallas_call | solution.py:85
  228.2 4.0 shard_map.75
  232.3 6.4 %collective-permute-done.34.got = bf16[896,256]{1,0:T(8,128)(2,1)S(1)} collective-permute-done((bf16[896,256]{1,0:T(8,128)(2,1)S(1)}, bf16[896,256]{1,0:T(8,128)(2,1)S(1)}, u32[]{:S(2)}, u32[]{:S(2)}) %collective-permute-start.34) | collective-permute-done | bytes 458784 | tf_op jit(solution)/shard_map/ppermute | solution.py:24
  250.5 4.8 %collective-permute-start.41 = (bf16[896,256]{1,0:T(8,128)(2,1)S(1)}, bf16[896,256]{1,0:T(8,128)(2,1)S(1)}, u32[]{:S(2)}, u32[]{:S(2)}) collective-permute-start(bf16[896,256]{1,0:T(8,128)(2,1)S(1)} %get-tuple-element.110.image), channel_id=1, source_target_pairs={{0,0},{1,4},{2,2},{3,6},{4,1},{5,5},{6,3},{7,7},{8,8},{9,12},{10,1... | collective-permute-start | bytes 1376264 | tf_op jit(solution)/shard_map/ppermute | solution.py:24
  260.4 6.3 %collective-permute-done.40 = f32[96,256]{1,0:T(8,128)S(1)} collective-permute-done((f32[96,256]{1,0:T(8,128)S(1)}, f32[96,256]{1,0:T(8,128)S(1)}, u32[]{:S(2)}, u32[]{:S(2)}) %collective-permute-start.40) | collective-permute-done | bytes 98336 | tf_op jit(solution)/shard_map/ppermute | solution.py:24
  276.4 11.3 %shard_map.77 = (f32[256,256]{1,0:T(8,128)S(1)}, f32[256,256]{1,0:T(8,128)S(1)}, f32[256,256]{1,0:T(8,128)S(1)}) custom-call(f32[768,256]{1,0:T(8,128)S(1)} %constant_dynamic-update-slice_fusion.12.grams, f32[256,256]{1,0:T(8,128)S(1)} %get-tuple-element.97.matrix.refs_0_, f32[256,256]{1,0:T(8,128)S(1)} %shard_map.69.refs_1_), custom_call_target="tpu_custom_call" | custom-call | flops 1677721600 | bytes 2097152 | tf_op jit(solution)/shard_map/pallas_call | solution.py:289
  287.7 6.5 %collective-permute-done.42.image = bf16[896,256]{1,0:T(8,128)(2,1)S(1)} collective-permute-done((bf16[896,256]{1,0:T(8,128)(2,1)S(1)}, bf16[896,256]{1,0:T(8,128)(2,1)S(1)}, u32[]{:S(2)}, u32[]{:S(2)}) %collective-permute-start.42) | collective-permute-done | bytes 458784 | tf_op jit(solution)/shard_map/ppermute | solution.py:24
  298.4 5.5 %shard_map.79.refs_4_ = f32[3584,256]{1,0:T(8,128)S(1)} custom-call(s32[12]{0:T(128)S(1)} %fusion.3.index_ref, bf16[3584,7168]{1,0:T(8,128)(2,1)} %refs_0_.35, bf16[896,256]{1,0:T(8,128)(2,1)S(1)} %get-tuple-element.116.refs_1_), custom_call_target="tpu_custom_call" | custom-call | flops 1644167168 | bytes 6422528 | tf_op jit(solution)/shard_map/pallas_call | solution.py:85
  309.8 9.5 %shard_map.81.refs_1_ = f32[256,256]{1,0:T(8,128)S(1)} custom-call(f32[256,256]{1,0:T(8,128)S(1)} %get-tuple-element.120.matrix.refs_0_), custom_call_target="tpu_custom_call" | custom-call | flops 1677721600 | bytes 524288 | tf_op jit(solution)/shard_map/pallas_call | solution.py:306
  319.3 8.0 %shard_map.80.refs_4_ = f32[3584,256]{1,0:T(8,128)S(1)} custom-call(s32[12]{0:T(128)S(1)} %fusion.3.index_ref, bf16[3584,7168]{1,0:T(8,128)(2,1)} %refs_0_.35, bf16[3584,7168]{1,0:T(8,128)(2,1)} %refs_0_.35, bf16[896,256]{1,0:T(8,128)(2,1)S(1)} %collective-permute-done.47.refs_2_, ...), custom_call_target="tpu_custom_call", output_to_operand_aliasing={{}: (5, {})} | custom-call | flops 3288334336 | bytes 12845056 | tf_op jit(solution)/shard_map/pallas_call | solution.py:85
  328.8 8.0 %shard_map.83.refs_4_ = f32[3584,256]{1,0:T(8,128)S(1)} custom-call(s32[12]{0:T(128)S(1)} %fusion.3.index_ref, bf16[3584,7168]{1,0:T(8,128)(2,1)} %refs_0_.35, bf16[3584,7168]{1,0:T(8,128)(2,1)} %refs_0_.35, bf16[896,256]{1,0:T(8,128)(2,1)S(1)} %collective-permute-done.49.refs_2_, ...), custom_call_target="tpu_custom_call", output_to_operand_aliasing={{}: (5, {})} | custom-call | flops 3288334336 | bytes 12845056 | tf_op jit(solution)/shard_map/pallas_call | solution.py:85
  340.0 8.0 %shard_map.84.refs_2_ = f32[3584,256]{1,0:T(8,128)S(1)} custom-call(s32[12]{0:T(128)S(1)} %fusion.3.index_ref, bf16[3584,7168]{1,0:T(8,128)(2,1)} %refs_0_.35, bf16[3584,7168]{1,0:T(8,128)(2,1)} %refs_0_.35, bf16[896,256]{1,0:T(8,128)(2,1)S(1)} %collective-permute-done.51.refs_2_, ...), custom_call_target="tpu_custom_call", output_to_operand_aliasing={{}: (5, {})} | custom-call | flops 3288334336 | bytes 12845056 | tf_op jit(solution)/shard_map/pallas_call | solution.py:85
  361.8 7.9 %collective-permute-done.57.got = bf16[896,256]{1,0:T(8,128)(2,1)S(1)} collective-permute-done((bf16[896,256]{1,0:T(8,128)(2,1)S(1)}, bf16[896,256]{1,0:T(8,128)(2,1)S(1)}, u32[]{:S(2)}, u32[]{:S(2)}) %collective-permute-start.57) | collective-permute-done | bytes 458784 | tf_op jit(solution)/shard_map/ppermute | solution.py:24
  390.6 6.7 %collective-permute-done.63 = f32[96,256]{1,0:T(8,128)S(1)} collective-permute-done((f32[96,256]{1,0:T(8,128)S(1)}, f32[96,256]{1,0:T(8,128)S(1)}, u32[]{:S(2)}, u32[]{:S(2)}) %collective-permute-start.63) | collective-permute-done | bytes 98336 | tf_op jit(solution)/shard_map/ppermute | solution.py:24
  407.8 11.6 %shard_map.89 = (f32[256,256]{1,0:T(8,128)S(1)}, f32[256,256]{1,0:T(8,128)S(1)}, f32[256,256]{1,0:T(8,128)}) custom-call(f32[768,256]{1,0:T(8,128)S(1)} %constant_dynamic-update-slice_fusion.6.grams, f32[256,256]{1,0:T(8,128)S(1)} %get-tuple-element.120.matrix.refs_0_, f32[256,256]{1,0:T(8,128)S(1)} %shard_map.81.refs_1_), custom_call_target="tpu_custom_call" | custom-call | flops 1677721600 | bytes 2097152 | tf_op jit(solution)/shard_map/pallas_call | solution.py:289
  421.3 4.1 collective-permute-done.69.image
  (236 shorter events, 177.5 us)
Async XLA Ops:
  1.9 12.4 %collective-permute-start = (bf16[896,256]{1,0:T(8,128)(2,1)S(1)}, bf16[896,256]{1,0:T(8,128)(2,1)S(1)}, u32[]{:S(2)}, u32[]{:S(2)}) collective-permute-start(bf16[896,256]{1,0:T(8,128)(2,1)S(1)} %convert_element_type.12.refs_1_), channel_id=1, source_target_pairs={{0,8},{1,9},{2,10},{3,11},{4,0},{5,1},{6,2},{7,3},{8,16},{9,17},{1... | collective-permute-start | bytes 1376264 | tf_op jit(solution)/shard_map/ppermute | solution.py:24
  4.0 11.1 %collective-permute-start.1 = (bf16[896,256]{1,0:T(8,128)(2,1)S(1)}, bf16[896,256]{1,0:T(8,128)(2,1)S(1)}, u32[]{:S(2)}, u32[]{:S(2)}) collective-permute-start(bf16[896,256]{1,0:T(8,128)(2,1)S(1)} %convert_element_type.12.refs_1_), channel_id=1, source_target_pairs={{8,0},{9,1},{10,2},{11,3},{0,4},{1,5},{2,6},{3,7},{16,8},{17,9},{1... | collective-permute-start | bytes 1376264 | tf_op jit(solution)/shard_map/ppermute | solution.py:24
  15.1 10.1 %collective-permute-start.2 = (bf16[896,256]{1,0:T(8,128)(2,1)S(1)}, bf16[896,256]{1,0:T(8,128)(2,1)S(1)}, u32[]{:S(2)}, u32[]{:S(2)}) collective-permute-start(bf16[896,256]{1,0:T(8,128)(2,1)S(1)} %collective-permute-done.refs_2_), channel_id=1, source_target_pairs={{0,8},{1,9},{2,10},{3,11},{4,0},{5,1},{6,2},{7,3},{8,16},{9,17},{1... | collective-permute-start | bytes 1376264 | tf_op jit(solution)/shard_map/ppermute | solution.py:24
  16.4 9.9 %collective-permute-start.3 = (bf16[896,256]{1,0:T(8,128)(2,1)S(1)}, bf16[896,256]{1,0:T(8,128)(2,1)S(1)}, u32[]{:S(2)}, u32[]{:S(2)}) collective-permute-start(bf16[896,256]{1,0:T(8,128)(2,1)S(1)} %collective-permute-done.1.refs_3_), channel_id=1, source_target_pairs={{8,0},{9,1},{10,2},{11,3},{0,4},{1,5},{2,6},{3,7},{16,8},{17,9},{1... | collective-permute-start | bytes 1376264 | tf_op jit(solution)/shard_map/ppermute | solution.py:24
  49.3 12.9 %collective-permute-start.9 = (f32[896,256]{1,0:T(8,128)S(1)}, f32[896,256]{1,0:T(8,128)S(1)}, u32[]{:S(2)}, u32[]{:S(2)}) collective-permute-start(f32[896,256]{1,0:T(8,128)S(1)} %slice.75), channel_id=1, source_target_pairs={{0,1},{1,0},{2,3},{3,2},{4,5},{5,4},{6,7},{7,6},{8,9},{9,8},{10,11... | collective-permute-start | bytes 2752520 | tf_op jit(solution)/shard_map/ppermute | solution.py:24
  58.5 15.0 %collective-permute-start.11 = (f32[896,256]{1,0:T(8,128)S(1)}, f32[896,256]{1,0:T(8,128)}, u32[]{:S(2)}, u32[]{:S(2)}) collective-permute-start(f32[896,256]{1,0:T(8,128)S(1)} %copy-done), channel_id=1, source_target_pairs={{0,0},{4,1},{8,2},{12,3},{16,4},{20,5},{24,6},{28,7},{1,8},{5,9},{... | collective-permute-start | bytes 2752520 | tf_op jit(solution)/shard_map/ppermute | solution.py:24
  63.0 30.5 %collective-permute-start.10 = (bf16[896,256]{1,0:T(8,128)(2,1)}, bf16[896,256]{1,0:T(8,128)(2,1)S(1)}, u32[]{:S(2)}, u32[]{:S(2)}) collective-permute-start(bf16[896,256]{1,0:T(8,128)(2,1)} %fusion.2), channel_id=1, source_target_pairs={{0,2},{1,3},{2,0},{3,1},{4,6},{5,7},{6,4},{7,5},{8,10},{9,11},{10,... | collective-permute-start | bytes 1376264 | tf_op jit(solution)/shard_map/ppermute | solution.py:24
  101.4 11.5 %collective-permute-start.13 = (f32[96,256]{1,0:T(8,128)S(1)}, f32[96,256]{1,0:T(8,128)S(1)}, u32[]{:S(2)}, u32[]{:S(2)}) collective-permute-start(f32[96,256]{1,0:T(8,128)S(1)} %get-tuple-element.151), channel_id=1, source_target_pairs={{0,2},{1,3},{2,0},{3,1},{4,6},{5,7},{6,4},{7,5},{8,10},{9,11},{10,... | collective-permute-start | bytes 294920 | tf_op jit(solution)/shard_map/ppermute | solution.py:24
  103.5 11.1 %collective-permute-start.14 = (f32[96,256]{1,0:T(8,128)S(1)}, f32[96,256]{1,0:T(8,128)S(1)}, u32[]{:S(2)}, u32[]{:S(2)}) collective-permute-start(f32[96,256]{1,0:T(8,128)S(1)} %get-tuple-element.153), channel_id=1, source_target_pairs={{0,4},{1,5},{2,6},{3,7},{4,0},{5,1},{6,2},{7,3},{8,12},{9,13},{10,... | collective-permute-start | bytes 294920 | tf_op jit(solution)/shard_map/ppermute | solution.py:24
  117.5 14.7 %collective-permute-start.18 = (bf16[896,256]{1,0:T(8,128)(2,1)S(1)}, bf16[896,256]{1,0:T(8,128)(2,1)S(1)}, u32[]{:S(2)}, u32[]{:S(2)}) collective-permute-start(bf16[896,256]{1,0:T(8,128)(2,1)S(1)} %get-tuple-element.86.image), channel_id=1, source_target_pairs={{0,0},{1,4},{2,2},{3,6},{4,1},{5,5},{6,3},{7,7},{8,8},{9,12},{10,1... | collective-permute-start | bytes 1376264 | tf_op jit(solution)/shard_map/ppermute | solution.py:24
  140.3 22.0 %collective-permute-start.19 = (bf16[896,256]{1,0:T(8,128)(2,1)S(1)}, bf16[896,256]{1,0:T(8,128)(2,1)S(1)}, u32[]{:S(2)}, u32[]{:S(2)}) collective-permute-start(bf16[896,256]{1,0:T(8,128)(2,1)S(1)} %collective-permute-done.18), channel_id=1, source_target_pairs={{0,0},{4,4},{2,8},{6,12},{1,16},{5,20},{3,24},{7,28},{8,1},{12,5},... | collective-permute-start | bytes 1376264 | tf_op jit(solution)/shard_map/ppermute | solution.py:24
  165.0 11.4 %collective-permute-start.24 = (bf16[896,256]{1,0:T(8,128)(2,1)S(1)}, bf16[896,256]{1,0:T(8,128)(2,1)S(1)}, u32[]{:S(2)}, u32[]{:S(2)}) collective-permute-start(bf16[896,256]{1,0:T(8,128)(2,1)S(1)} %get-tuple-element.93.refs_1_), channel_id=1, source_target_pairs={{0,8},{1,9},{2,10},{3,11},{4,0},{5,1},{6,2},{7,3},{8,16},{9,17},{1... | collective-permute-start | bytes 1376264 | tf_op jit(solution)/shard_map/ppermute | solution.py:24
  165.3 11.5 %collective-permute-start.25 = (bf16[896,256]{1,0:T(8,128)(2,1)S(1)}, bf16[896,256]{1,0:T(8,128)(2,1)S(1)}, u32[]{:S(2)}, u32[]{:S(2)}) collective-permute-start(bf16[896,256]{1,0:T(8,128)(2,1)S(1)} %get-tuple-element.93.refs_1_), channel_id=1, source_target_pairs={{8,0},{9,1},{10,2},{11,3},{0,4},{1,5},{2,6},{3,7},{16,8},{17,9},{1... | collective-permute-start | bytes 1376264 | tf_op jit(solution)/shard_map/ppermute | solution.py:24
  176.9 18.4 %collective-permute-start.26 = (bf16[896,256]{1,0:T(8,128)(2,1)S(1)}, bf16[896,256]{1,0:T(8,128)(2,1)S(1)}, u32[]{:S(2)}, u32[]{:S(2)}) collective-permute-start(bf16[896,256]{1,0:T(8,128)(2,1)S(1)} %collective-permute-done.24.refs_2_), channel_id=1, source_target_pairs={{0,8},{1,9},{2,10},{3,11},{4,0},{5,1},{6,2},{7,3},{8,16},{9,17},{1... | collective-permute-start | bytes 1376264 | tf_op jit(solution)/shard_map/ppermute | solution.py:24
  177.2 18.0 %collective-permute-start.27 = (bf16[896,256]{1,0:T(8,128)(2,1)S(1)}, bf16[896,256]{1,0:T(8,128)(2,1)S(1)}, u32[]{:S(2)}, u32[]{:S(2)}) collective-permute-start(bf16[896,256]{1,0:T(8,128)(2,1)S(1)} %collective-permute-done.25.refs_3_), channel_id=1, source_target_pairs={{8,0},{9,1},{10,2},{11,3},{0,4},{1,5},{2,6},{3,7},{16,8},{17,9},{1... | collective-permute-start | bytes 1376264 | tf_op jit(solution)/shard_map/ppermute | solution.py:24
  195.3 10.1 %collective-permute-start.28 = (bf16[896,256]{1,0:T(8,128)(2,1)S(1)}, bf16[896,256]{1,0:T(8,128)(2,1)S(1)}, u32[]{:S(2)}, u32[]{:S(2)}) collective-permute-start(bf16[896,256]{1,0:T(8,128)(2,1)S(1)} %collective-permute-done.26.refs_2_), channel_id=1, source_target_pairs={{0,8},{1,9},{2,10},{3,11},{4,0},{5,1},{6,2},{7,3},{8,16},{9,17},{1... | collective-permute-start | bytes 1376264 | tf_op jit(solution)/shard_map/ppermute | solution.py:24
  195.7 10.1 %collective-permute-start.29 = (bf16[896,256]{1,0:T(8,128)(2,1)S(1)}, bf16[896,256]{1,0:T(8,128)(2,1)S(1)}, u32[]{:S(2)}, u32[]{:S(2)}) collective-permute-start(bf16[896,256]{1,0:T(8,128)(2,1)S(1)} %collective-permute-done.27.refs_3_), channel_id=1, source_target_pairs={{8,0},{9,1},{10,2},{11,3},{0,4},{1,5},{2,6},{3,7},{16,8},{17,9},{1... | collective-permute-start | bytes 1376264 | tf_op jit(solution)/shard_map/ppermute | solution.py:24
  205.8 10.4 %collective-permute-start.30 = (bf16[448,256]{1,0:T(8,128)(2,1)S(1)}, bf16[448,256]{1,0:T(8,128)(2,1)S(1)}, u32[]{:S(2)}, u32[]{:S(2)}) collective-permute-start(bf16[448,256]{1,0:T(8,128)(2,1)S(1)} %slice.60), channel_id=1, source_target_pairs={{0,8},{1,9},{2,10},{3,11},{4,0},{5,1},{6,2},{7,3},{8,16},{9,17},{1... | collective-permute-start | bytes 688136 | tf_op jit(solution)/shard_map/ppermute | solution.py:24
  206.1 10.0 %collective-permute-start.31 = (bf16[448,256]{1,0:T(8,128)(2,1)S(1)}, bf16[448,256]{1,0:T(8,128)(2,1)S(1)}, u32[]{:S(2)}, u32[]{:S(2)}) collective-permute-start(bf16[448,256]{1,0:T(8,128)(2,1)S(1)} %slice.61), channel_id=1, source_target_pairs={{8,0},{9,1},{10,2},{11,3},{0,4},{1,5},{2,6},{3,7},{16,8},{17,9},{1... | collective-permute-start | bytes 688136 | tf_op jit(solution)/shard_map/ppermute | solution.py:24
  226.1 12.6 %collective-permute-start.34 = (bf16[896,256]{1,0:T(8,128)(2,1)S(1)}, bf16[896,256]{1,0:T(8,128)(2,1)S(1)}, u32[]{:S(2)}, u32[]{:S(2)}) collective-permute-start(bf16[896,256]{1,0:T(8,128)(2,1)S(1)} %fusion.1), channel_id=1, source_target_pairs={{0,2},{1,3},{2,0},{3,1},{4,6},{5,7},{6,4},{7,5},{8,10},{9,11},{10,... | collective-permute-start | bytes 1376264 | tf_op jit(solution)/shard_map/ppermute | solution.py:24
  250.5 16.2 %collective-permute-start.41 = (bf16[896,256]{1,0:T(8,128)(2,1)S(1)}, bf16[896,256]{1,0:T(8,128)(2,1)S(1)}, u32[]{:S(2)}, u32[]{:S(2)}) collective-permute-start(bf16[896,256]{1,0:T(8,128)(2,1)S(1)} %get-tuple-element.110.image), channel_id=1, source_target_pairs={{0,0},{1,4},{2,2},{3,6},{4,1},{5,5},{6,3},{7,7},{8,8},{9,12},{10,1... | collective-permute-start | bytes 1376264 | tf_op jit(solution)/shard_map/ppermute | solution.py:24
  274.3 19.9 %collective-permute-start.42 = (bf16[896,256]{1,0:T(8,128)(2,1)S(1)}, bf16[896,256]{1,0:T(8,128)(2,1)S(1)}, u32[]{:S(2)}, u32[]{:S(2)}) collective-permute-start(bf16[896,256]{1,0:T(8,128)(2,1)S(1)} %collective-permute-done.41), channel_id=1, source_target_pairs={{0,0},{4,4},{2,8},{6,12},{1,16},{5,20},{3,24},{7,28},{8,1},{12,5},... | collective-permute-start | bytes 1376264 | tf_op jit(solution)/shard_map/ppermute | solution.py:24
  296.0 10.3 %collective-permute-start.47 = (bf16[896,256]{1,0:T(8,128)(2,1)S(1)}, bf16[896,256]{1,0:T(8,128)(2,1)S(1)}, u32[]{:S(2)}, u32[]{:S(2)}) collective-permute-start(bf16[896,256]{1,0:T(8,128)(2,1)S(1)} %get-tuple-element.116.refs_1_), channel_id=1, source_target_pairs={{0,8},{1,9},{2,10},{3,11},{4,0},{5,1},{6,2},{7,3},{8,16},{9,17},{1... | collective-permute-start | bytes 1376264 | tf_op jit(solution)/shard_map/ppermute | solution.py:24
  296.1 12.3 %collective-permute-start.48 = (bf16[896,256]{1,0:T(8,128)(2,1)S(1)}, bf16[896,256]{1,0:T(8,128)(2,1)S(1)}, u32[]{:S(2)}, u32[]{:S(2)}) collective-permute-start(bf16[896,256]{1,0:T(8,128)(2,1)S(1)} %get-tuple-element.116.refs_1_), channel_id=1, source_target_pairs={{8,0},{9,1},{10,2},{11,3},{0,4},{1,5},{2,6},{3,7},{16,8},{17,9},{1... | collective-permute-start | bytes 1376264 | tf_op jit(solution)/shard_map/ppermute | solution.py:24
  308.3 19.0 %collective-permute-start.49 = (bf16[896,256]{1,0:T(8,128)(2,1)S(1)}, bf16[896,256]{1,0:T(8,128)(2,1)S(1)}, u32[]{:S(2)}, u32[]{:S(2)}) collective-permute-start(bf16[896,256]{1,0:T(8,128)(2,1)S(1)} %collective-permute-done.47.refs_2_), channel_id=1, source_target_pairs={{0,8},{1,9},{2,10},{3,11},{4,0},{5,1},{6,2},{7,3},{8,16},{9,17},{1... | collective-permute-start | bytes 1376264 | tf_op jit(solution)/shard_map/ppermute | solution.py:24
  308.5 18.8 %collective-permute-start.50 = (bf16[896,256]{1,0:T(8,128)(2,1)S(1)}, bf16[896,256]{1,0:T(8,128)(2,1)S(1)}, u32[]{:S(2)}, u32[]{:S(2)}) collective-permute-start(bf16[896,256]{1,0:T(8,128)(2,1)S(1)} %collective-permute-done.48.refs_3_), channel_id=1, source_target_pairs={{8,0},{9,1},{10,2},{11,3},{0,4},{1,5},{2,6},{3,7},{16,8},{17,9},{1... | collective-permute-start | bytes 1376264 | tf_op jit(solution)/shard_map/ppermute | solution.py:24
  327.3 10.8 %collective-permute-start.51 = (bf16[896,256]{1,0:T(8,128)(2,1)S(1)}, bf16[896,256]{1,0:T(8,128)(2,1)S(1)}, u32[]{:S(2)}, u32[]{:S(2)}) collective-permute-start(bf16[896,256]{1,0:T(8,128)(2,1)S(1)} %collective-permute-done.49.refs_2_), channel_id=1, source_target_pairs={{0,8},{1,9},{2,10},{3,11},{4,0},{5,1},{6,2},{7,3},{8,16},{9,17},{1... | collective-permute-start | bytes 1376264 | tf_op jit(solution)/shard_map/ppermute | solution.py:24
  327.5 10.7 %collective-permute-start.52 = (bf16[896,256]{1,0:T(8,128)(2,1)S(1)}, bf16[896,256]{1,0:T(8,128)(2,1)S(1)}, u32[]{:S(2)}, u32[]{:S(2)}) collective-permute-start(bf16[896,256]{1,0:T(8,128)(2,1)S(1)} %collective-permute-done.50.refs_3_), channel_id=1, source_target_pairs={{8,0},{9,1},{10,2},{11,3},{0,4},{1,5},{2,6},{3,7},{16,8},{17,9},{1... | collective-permute-start | bytes 1376264 | tf_op jit(solution)/shard_map/ppermute | solution.py:24
  338.2 9.8 %collective-permute-start.53 = (bf16[448,256]{1,0:T(8,128)(2,1)S(1)}, bf16[448,256]{1,0:T(8,128)(2,1)S(1)}, u32[]{:S(2)}, u32[]{:S(2)}) collective-permute-start(bf16[448,256]{1,0:T(8,128)(2,1)S(1)} %slice.66), channel_id=1, source_target_pairs={{0,8},{1,9},{2,10},{3,11},{4,0},{5,1},{6,2},{7,3},{8,16},{9,17},{1... | collective-permute-start | bytes 688136 | tf_op jit(solution)/shard_map/ppermute | solution.py:24
  358.0 11.7 %collective-permute-start.57 = (bf16[896,256]{1,0:T(8,128)(2,1)S(1)}, bf16[896,256]{1,0:T(8,128)(2,1)S(1)}, u32[]{:S(2)}, u32[]{:S(2)}) collective-permute-start(bf16[896,256]{1,0:T(8,128)(2,1)S(1)} %fusion), channel_id=1, source_target_pairs={{0,2},{1,3},{2,0},{3,1},{4,6},{5,7},{6,4},{7,5},{8,10},{9,11},{10,... | collective-permute-start | bytes 1376264 | tf_op jit(solution)/shard_map/ppermute | solution.py:24
  382.7 14.6 %collective-permute-start.64 = (bf16[896,256]{1,0:T(8,128)(2,1)S(1)}, bf16[896,256]{1,0:T(8,128)(2,1)S(1)}, u32[]{:S(2)}, u32[]{:S(2)}) collective-permute-start(bf16[896,256]{1,0:T(8,128)(2,1)S(1)} %get-tuple-element.136), channel_id=1, source_target_pairs={{0,0},{1,4},{2,2},{3,6},{4,1},{5,5},{6,3},{7,7},{8,8},{9,12},{10,1... | collective-permute-start | bytes 1376264 | tf_op jit(solution)/shard_map/ppermute | solution.py:24
  405.8 19.6 %collective-permute-start.69 = (bf16[896,256]{1,0:T(8,128)(2,1)S(1)}, bf16[896,256]{1,0:T(8,128)(2,1)S(1)}, u32[]{:S(2)}, u32[]{:S(2)}) collective-permute-start(bf16[896,256]{1,0:T(8,128)(2,1)S(1)} %collective-permute-done.64), channel_id=1, source_target_pairs={{0,0},{4,4},{2,8},{6,12},{1,16},{5,20},{3,24},{7,28},{8,1},{12,5},... | collective-permute-start | bytes 1376264 | tf_op jit(solution)/shard_map/ppermute | solution.py:24
  (51 other events, 289.7 us)
